TPU v7x, 128 devices: a whole 4x4x4 slice. The times are simulated.
128 devices in a mesh: engine: 4 (over y), tp: 32 (over x, z, core).
Axes of the slice: x: 4, y: 4, z: 4, core: 2. Of those that a mesh axis runs over, the one named last changes fastest.
Arguments:
- trainer_panels: bfloat16 [256, 64, 18432], P(('engine', 'tp')), may hold values from -1 to 1
- panel_ids: int32 [256], P(('engine', 'tp')), may hold values from 0 to 128, as said below
- first_tokens: bfloat16 [512, 8192], P('engine'), may hold values from -6 to 6
- second_tokens: bfloat16 [512, 8192], P('engine'), may hold values from -6 to 6
- norm_gain: float32 [8192], replicated, may hold values from 0.5 to 1.5
- kv_cache: bfloat16 [4, 768, 128, 2048], P('engine', 'tp'), may hold values from -6 to 6
- block_table: int32 [512, 6], P(('engine', 'tp')), may hold values from 0 to 23, as said below
- lengths: int32 [512], P(('engine', 'tp')), may hold values from 4 to 766
- move_list: int32 [4, 32, 4, 1], P('engine', 'tp'), may hold values from 0 to 24, as said below
Outputs:
- first_out: bfloat16 [512, 8192], P('engine', 'tp')
- second_out: bfloat16 [512, 8192], P('engine', 'tp')
- hosted: bfloat16 [4, 128, 128, 2048], P('engine', 'tp')
Inputs may be any that keep to these rules, and one draw needn't show every extreme that they name: `panel_ids`: every panel 0 to 127 stands in exactly one slot; the other slots hold 128; the slots of some device are all full. `block_table`: the entries of one device's rollouts list each of its 24 blocks once. `move_list`: A device never names a block for its own engine, and names each block at most once.
All inputs are finite; a program needn't handle non-finite values.
Results may differ from a plain program's by a relative error of at most 0.02.
Values may be sent and summed in bfloat16 or wider, within the bound.
No kernel may reach another device: no remote copies, remote signals or barrier semaphores. Data moves between devices by JAX's collectives and lax.ppermute only.
A program may use at most 256 MiB of HBM per device.

v0:
```python
import math

import jax
import jax.numpy as jnp
from jax import lax
from jax.experimental import pallas as pl
from jax.experimental.pallas import tpu as pltpu
from jax.sharding import Mesh
from jax.sharding import PartitionSpec as P

D = 8192
KVH = 8
HD = 128
PANELS = 128
BLK = 128
MAXB = 6
NBLK = 24
KV = KVH * HD
QKV = D + 2 * KV
GROUP = 1280
PR = 64
BF = jnp.bfloat16
F32 = jnp.float32
ROWS = 16
VMEM = 60 * 2**20


def shift(v, axis, k):
    return lax.ppermute(v, axis, [(i, (i + k) % 4) for i in range(4)])


def swap(v):
    return lax.ppermute(v, "c", [(0, 1), (1, 0)])


def split_kernel(q_ref, k_ref, v_ref, out_ref):
    for s in range(2):
        rows = slice(s * PR, (s + 1) * PR)
        out_ref[0, rows, :1024] = q_ref[s]
        out_ref[0, rows, 1024 : 1024 + HD] = k_ref[s]
        out_ref[0, rows, 1024 + HD :] = v_ref[s]


def split_heads(panels):
    return pl.pallas_call(
        split_kernel,
        grid=(KVH,),
        in_specs=[
            pl.BlockSpec((2, PR, 1024), lambda g: (0, 0, g)),
            pl.BlockSpec((2, PR, HD), lambda g: (0, 0, D // HD + g)),
            pl.BlockSpec((2, PR, HD), lambda g: (0, 0, (D + KV) // HD + g)),
        ],
        out_specs=pl.BlockSpec((1, 2 * PR, GROUP), lambda g: (g, 0, 0)),
        out_shape=jax.ShapeDtypeStruct((KVH, 2 * PR, GROUP), BF),
        cost_estimate=pl.CostEstimate(flops=0, bytes_accessed=5_300_000, transcendentals=0),
        name="split_heads",
    )(panels, panels, panels)


def pick_kernel(ids_ref, at_ref, first_ref, second_ref, gain_ref, out_ref, x_ref, scale_ref):
    e = pl.program_id(0)

    @pl.when(e == 0)
    def _():
        x = jnp.concatenate([first_ref[...].astype(F32), second_ref[...].astype(F32)], axis=0)
        x_ref[...] = x
        mean = jnp.mean(x * x, axis=-1, keepdims=True)
        scale_ref[...] = jnp.broadcast_to(lax.rsqrt(mean + 1e-06), (32, 128))

    lane = lax.broadcasted_iota(jnp.int32, (32, 128), 1)
    scale = scale_ref[...]
    new = lax.broadcasted_iota(jnp.int32, (32, 32), 0)
    old = lax.broadcasted_iota(jnp.int32, (32, 32), 1)
    source = ((new // 4) % 2) * 16 + (new // 8) * 4 + new % 4
    turn = (old == source).astype(BF)

    def column(slot):
        p = ids_ref[e * 16 + slot]
        valid = p < PANELS
        p = jnp.where(valid, p, 0)
        at = pl.multiple_of((p // 2) * 128, 128)
        v = x_ref[:, pl.ds(at, 128)] * scale * gain_ref[:, pl.ds(at, 128)]
        return jnp.where(valid, v, 0.0), p % 2

    for pair in range(8):
        a, odd_a = column(2 * pair)
        b, odd_b = column(2 * pair + 1)
        a = jnp.where(odd_a == 1, pltpu.roll(a, 64, 1), a)
        b = jnp.where(odd_b == 0, pltpu.roll(b, 64, 1), b)
        both = jnp.where(lane < 64, a, b).astype(BF)
        both = jnp.dot(turn, both, preferred_element_type=F32).astype(BF)
        for z in range(4):
            out_ref[0, z, :, pair * 128 : (pair + 1) * 128] = both


def pick_columns(ids, at, first, second, gain):
    return pl.pallas_call(
        pick_kernel,
        grid_spec=pltpu.PrefetchScalarGridSpec(
            num_scalar_prefetch=2,
            grid=(4,),
            in_specs=[
                pl.BlockSpec((16, D), lambda e, ids, at: (at[0], 0)),
                pl.BlockSpec((16, D), lambda e, ids, at: (at[0], 0)),
                pl.BlockSpec((1, D), lambda e, ids, at: (0, 0)),
            ],
            out_specs=pl.BlockSpec((1, 4, 32, 1024), lambda e, ids, at: (e, 0, 0, 0)),
            scratch_shapes=[pltpu.VMEM((32, D), F32), pltpu.VMEM((32, 128), F32)],
        ),
        out_shape=jax.ShapeDtypeStruct((4, 4, 32, 1024), BF),
        cost_estimate=pl.CostEstimate(flops=20_000_000, bytes_accessed=2_000_000, transcendentals=0),
        name="pick_columns",
    )(ids, at, first, second, gain)


def attend_kernel(table_ref, length_ref, q_ref, k_ref, v_ref, *refs):
    blocks, out_ref = refs[:MAXB], refs[MAXB]
    r = pl.program_id(0)
    length = length_ref[r]
    inverse_root = 1.0 / math.sqrt(HD)
    row = lax.broadcasted_iota(jnp.int32, (16, 128), 0)
    lane = lax.broadcasted_iota(jnp.int32, (16, 128), 1)
    fresh_seen = jnp.logical_or(lane == 0, jnp.logical_and(lane == 1, row >= 8))
    nt = (((1,), (1,)), ((), ()))
    pad = jnp.zeros((126, HD), F32)
    for g in range(KVH):
        lo = g * HD
        q = q_ref[0, g]
        new_k = jnp.concatenate([k_ref[0, :, lo : lo + HD].astype(F32), pad], axis=0).astype(BF)
        new_v = jnp.concatenate([v_ref[0, :, lo : lo + HD].astype(F32), pad], axis=0).astype(BF)
        scores = []
        for b in range(MAXB):
            keys = blocks[b][0, :, 2 * lo : 2 * lo + HD]
            s = lax.dot_general(q, keys, nt, preferred_element_type=F32) * inverse_root
            scores.append(jnp.where(lane + b * BLK < length, s, -1e30))
        s = lax.dot_general(q, new_k, nt, preferred_element_type=F32) * inverse_root
        scores.append(jnp.where(fresh_seen, s, -1e30))
        top = scores[0]
        for s in scores[1:]:
            top = jnp.maximum(top, s)
        top = jnp.max(top, axis=1, keepdims=True)
        weights = [jnp.exp(s - top) for s in scores]
        total = weights[0]
        for p in weights[1:]:
            total = total + p
        total = jnp.sum(total, axis=1, keepdims=True)
        inverse = 1.0 / total
        mixed = jnp.dot((weights[MAXB] * inverse).astype(BF), new_v, preferred_element_type=F32)
        for b in range(MAXB):
            vals = blocks[b][0, :, 2 * lo + HD : 2 * lo + 2 * HD]
            mixed += jnp.dot((weights[b] * inverse).astype(BF), vals, preferred_element_type=F32)
        out_ref[0, g] = mixed.astype(BF)


def attend(table, length, q, k, v, cache):
    def block(b):
        return pl.BlockSpec((1, BLK, 2 * KV), lambda r, t, n: (t[r * MAXB + b], 0, 0))

    return pl.pallas_call(
        attend_kernel,
        grid_spec=pltpu.PrefetchScalarGridSpec(
            num_scalar_prefetch=2,
            grid=(4,),
            in_specs=[
                pl.BlockSpec((1, KVH, 16, HD), lambda r, t, n: (r, 0, 0, 0)),
                pl.BlockSpec((1, 2, KV), lambda r, t, n: (r, 0, 0)),
                pl.BlockSpec((1, 2, KV), lambda r, t, n: (r, 0, 0)),
                *[block(b) for b in range(MAXB)],
            ],
            out_specs=pl.BlockSpec((1, KVH, 16, HD), lambda r, t, n: (r, 0, 0, 0)),
        ),
        out_shape=jax.ShapeDtypeStruct((4, KVH, 16, HD), BF),
        compiler_params=pltpu.CompilerParams(vmem_limit_bytes=VMEM),
        cost_estimate=pl.CostEstimate(flops=200_000_000, bytes_accessed=13_000_000, transcendentals=400_000),
        name="attend",
    )(table, length, q, k, v, *[cache] * MAXB)


def move_kernel(want_ref, table_ref, length_ref, fresh_ref, block_ref, out_ref):
    i = pl.program_id(0)
    b = want_ref[i]
    valid = b < NBLK
    out_ref[...] = jnp.where(valid, block_ref[...], jnp.zeros_like(block_ref))
    row = lax.broadcasted_iota(jnp.int32, (BLK, 2 * KV), 0)
    for r in range(4):
        for s in range(2):
            at = length_ref[r] + s
            hit = table_ref[r * MAXB + at // BLK] == b

            @pl.when(hit)
            def _(r=r, s=s, at=at):
                line = fresh_ref[2 * r + s : 2 * r + s + 1, :].astype(F32)
                old = out_ref[0].astype(F32)
                out_ref[0] = jnp.where(row == at % BLK, line, old).astype(BF)


def moved_blocks(want, table, length, fresh, cache):
    return pl.pallas_call(
        move_kernel,
        grid_spec=pltpu.PrefetchScalarGridSpec(
            num_scalar_prefetch=3,
            grid=(3,),
            in_specs=[
                pl.BlockSpec((8, 2 * KV), lambda i, w, t, n: (0, 0)),
                pl.BlockSpec((1, BLK, 2 * KV), lambda i, w, t, n: (jnp.minimum(w[i], NBLK - 1), 0, 0)),
            ],
            out_specs=pl.BlockSpec((1, BLK, 2 * KV), lambda i, w, t, n: (i, 0, 0)),
        ),
        out_shape=jax.ShapeDtypeStruct((3, BLK, 2 * KV), BF),
        compiler_params=pltpu.CompilerParams(vmem_limit_bytes=VMEM),
        cost_estimate=pl.CostEstimate(flops=1_000_000, bytes_accessed=3_200_000, transcendentals=0),
        name="moved_blocks",
    )(want, table, length, fresh, cache)


def order_kernel(from_ref, at_ref, half_ref, in_ref, out_ref):
    lane = lax.broadcasted_iota(jnp.int32, (8, 128), 1)

    def side(p, here):
        at = pl.multiple_of(at_ref[p] * 128, 128)
        v = in_ref[from_ref[p], :, pl.ds(at, 128)].astype(F32)
        return jnp.where(half_ref[p] == here, v, pltpu.roll(v, 64, 1))

    def step(q, _):
        for s in range(2):
            pair = 2 * q + s
            both = jnp.where(lane < 64, side(2 * pair, 0), side(2 * pair + 1, 1))
            out_ref[q, :, s * 128 : (s + 1) * 128] = both.astype(BF)
        return 0

    lax.fori_loop(0, 32, step, 0)


def panel_order(source, at, half, arrived):
    return pl.pallas_call(
        order_kernel,
        grid_spec=pltpu.PrefetchScalarGridSpec(
            num_scalar_prefetch=3,
            grid=(1,),
            in_specs=[pl.BlockSpec((32, 8, 512), lambda i, f, a, h: (0, 0, 0))],
            out_specs=pl.BlockSpec((32, 8, 256), lambda i, f, a, h: (0, 0, 0)),
        ),
        out_shape=jax.ShapeDtypeStruct((32, 8, 256), BF),
        name="panel_order",
    )(source, at, half, arrived)


def per_device(panels, panel_ids, first, second, gain, kv_cache, block_table, lengths, move_list):
    y, x = lax.axis_index("y"), lax.axis_index("x")
    z, c = lax.axis_index("z"), lax.axis_index("c")
    cache = kv_cache[0]
    table = block_table.reshape(-1)
    plane = ("x", "z", "c")

    w_o = lax.all_gather(panels[:, :, QKV:], "y", axis=0, tiled=True).reshape(8 * PR, D)

    ids = lax.all_to_all(
        jnp.broadcast_to(panel_ids[None], (128, 2)), ("y", "x", "z", "c"), 0, 0, tiled=True
    )
    near = lax.dynamic_index_in_dim(ids.reshape(4, 4, 16), x, 1, keepdims=False).reshape(64)

    w_in = lax.all_to_all(split_heads(panels), ("z", "c"), 0, 0, tiled=True).reshape(16 * PR, GROUP)

    block = (z * 2 + c).reshape(1)
    picked = pick_columns(near, block, first, second, gain.reshape(1, D))
    rows = lax.all_to_all(picked.reshape(16, 32, 1024), ("y", "z"), 0, 0, tiled=True)
    other = swap(rows)
    rows = jnp.where(
        c == 0, jnp.stack([rows, other], axis=1), jnp.stack([other, rows], axis=1)
    ).reshape(64 * ROWS, 1024)
    partial = jnp.dot(rows, w_in, preferred_element_type=F32).astype(BF)
    parts = lax.all_to_all(partial.reshape(16, 64, GROUP), ("y", "x"), 0, 0, tiled=True)
    summed = jnp.sum(parts.astype(F32), axis=0).astype(BF)
    projected = lax.all_to_all(summed.reshape(8, 8, GROUP), ("z", "c"), 0, 0, tiled=True)
    projected = projected.reshape(KVH, 2, 4, GROUP)
    query = projected[..., :1024].reshape(KVH, 2, 4, 8, HD).transpose(2, 0, 1, 3, 4)
    query = query.reshape(4, KVH, 16, HD)
    fresh = projected[..., 1024:].transpose(2, 1, 0, 3)
    new_k = fresh[..., :HD].reshape(4, 2, KV)
    new_v = fresh[..., HD:].reshape(4, 2, KV)
    fresh = fresh.reshape(8, 2 * KV)

    want = move_list.reshape(4)
    want = jnp.stack([lax.dynamic_index_in_dim(want, (y + k) % 4, 0, keepdims=False) for k in (1, 2, 3)])
    moving = moved_blocks(want, table, lengths, fresh, cache)
    got = [shift(moving[k - 1], "y", k) for k in (1, 2, 3)]

    mixed = attend(table, lengths, query, new_k, new_v, cache)
    mixed = mixed.reshape(4, KVH, 2, 8, HD).transpose(2, 0, 1, 3, 4).reshape(8, D)
    mixed = lax.all_gather(mixed, plane, axis=0, tiled=True)
    out = lax.dot_general(mixed, w_o, (((1,), (1,)), ((), ())), preferred_element_type=F32)

    arrived = lax.all_to_all(out.astype(BF).reshape(32, 8, 512), plane, 0, 0, tiled=True)
    match = ids.reshape(1, 256) == jnp.arange(PANELS, dtype=jnp.int32)[:, None]
    slot = jnp.sum(jnp.where(match, jnp.arange(256, dtype=jnp.int32)[None, :], 0), axis=1)
    ordered = panel_order((slot // 2) % 32, slot // 64, slot % 2, arrived)
    final = lax.all_to_all(ordered, plane, 0, 0, tiled=True).reshape(32, 2, 4, 256)

    hosted = jnp.zeros((4, BLK, 2 * KV), BF)
    for k in (1, 2, 3):
        hosted = lax.dynamic_update_index_in_dim(hosted, got[k - 1], (y + 4 - k) % 4, 0)
    return final[:, 0].reshape(128, 256), final[:, 1].reshape(128, 256), hosted[None]


def solution(mesh):
    grid = Mesh(mesh.devices.reshape(4, 4, 4, 2), ("y", "x", "z", "c"))
    every, plane = ("y", "x", "z", "c"), ("x", "z", "c")
    placed = (
        P(every, None, None),
        P(every),
        P("y", None),
        P("y", None),
        P(),
        P("y", plane, None, None),
        P(every, None),
        P(every),
        P("y", plane, None, None),
    )
    return jax.shard_map(
        per_device,
        mesh=grid,
        in_specs=placed,
        out_specs=(P("y", plane), P("y", plane), P("y", plane, None, None)),
        check_vma=False,
    )
```

profile of v0, /device:TPU:1, one launch (start us, length us, event | category | flops | bytes accessed | tf_op | source)
XLA Modules:
  0.0 272.3 jit_solution(14065446073103134019)
XLA Ops:
  7.2 3.1 %slice.34 = bf16[2,64,8192]{2,1,0:T(8,128)(2,1)} slice(bf16[2,64,18432]{2,1,0:T(8,128)(2,1)} %v_ref.1), slice={[0:2], [0:64], [10240:18432]} | slice | bytes 4194304 | tf_op jit(solution)/shard_map/slice | solution.py:255
  11.6 11.5 %all-to-all-start = ((s32[128,1,2]{2,1,0:T(1,128)}), s32[128,1,2]{2,1,0:T(1,128)S(1)}, u32[]{:S(2)}, u32[]{:S(2)}) async-start(s32[128,1,2]{2,1,0:T(1,128)} %broadcast_in_dim.34), calls=%async_computation | async-start | bytes 131072 | tf_op jit(solution)/shard_map/all_to_all | solution.py:257
  23.1 9.3 %all-to-all-done = s32[128,1,2]{2,1,0:T(1,128)S(1)} async-done(((s32[128,1,2]{2,1,0:T(1,128)}), s32[128,1,2]{2,1,0:T(1,128)S(1)}, u32[]{:S(2)}, u32[]{:S(2)}) %all-to-all-start) | async-done | bytes 1056 | tf_op jit(solution)/shard_map/all_to_all | solution.py:257
  33.2 4.4 %pick_columns.1 = bf16[4,4,32,1024]{3,2,1,0:T(8,128)(2,1)} custom-call(s32[64]{0:T(128)} %reshape.105.ids_ref, s32[1]{0:T(128)} %bitcast.at_ref, bf16[128,8192]{1,0:T(8,128)(2,1)} %first_ref.1, bf16[128,8192]{1,0:T(8,128)(2,1)} %second_ref.1, f32[1,8192]{1,0:T(1,128)} %bitcast.79), custom_call_target="tpu_custom_call" | custom-call | flops 20000000 | bytes 2000000 | tf_op jit(solution)/shard_map/pick_columns/pallas_call | solution.py:97
  37.6 3.7 %all-to-all-start.1 = ((bf16[16,32,1024]{2,1,0:T(8,128)(2,1)}), bf16[16,32,1024]{2,1,0:T(8,128)(2,1)S(1)}, u32[]{:S(2)}, u32[]{:S(2)}) async-start(bf16[16,32,1024]{2,1,0:T(8,128)(2,1)} %bitcast.69), calls=%async_computation.1 | async-start | bytes 2097152 | tf_op jit(solution)/shard_map/all_to_all | solution.py:266
  41.2 6.0 %split_heads.1 = bf16[8,128,1280]{2,1,0:T(8,128)(2,1)} custom-call(bf16[2,64,18432]{2,1,0:T(8,128)(2,1)} %v_ref.1, bf16[2,64,18432]{2,1,0:T(8,128)(2,1)} %v_ref.1, bf16[2,64,18432]{2,1,0:T(8,128)(2,1)} %v_ref.1), custom_call_target="tpu_custom_call" | custom-call | bytes 5300000 | tf_op jit(solution)/shard_map/split_heads/pallas_call | solution.py:45
  47.2 18.3 %all-to-all-done.1 = bf16[16,32,1024]{2,1,0:T(8,128)(2,1)S(1)} async-done(((bf16[16,32,1024]{2,1,0:T(8,128)(2,1)}), bf16[16,32,1024]{2,1,0:T(8,128)(2,1)S(1)}, u32[]{:S(2)}, u32[]{:S(2)}) %all-to-all-start.1) | async-done | bytes 1048608 | tf_op jit(solution)/shard_map/all_to_all | solution.py:266
  65.5 8.1 %all-to-all-start.2 = ((bf16[8,128,1280]{2,1,0:T(8,128)(2,1)}), bf16[8,128,1280]{2,1,0:T(8,128)(2,1)}, u32[]{:S(2)}, u32[]{:S(2)}) async-start(bf16[8,128,1280]{2,1,0:T(8,128)(2,1)} %split_heads.1), calls=%async_computation.2 | async-start | bytes 5242880 | tf_op jit(solution)/shard_map/all_to_all | solution.py:262
  73.7 2.7 %collective-permute-done = bf16[16,32,1024]{2,1,0:T(8,128)(2,1)S(1)} collective-permute-done((bf16[16,32,1024]{2,1,0:T(8,128)(2,1)S(1)}, bf16[16,32,1024]{2,1,0:T(8,128)(2,1)S(1)}, u32[]{:S(2)}, u32[]{:S(2)}) %collective-permute-start) | collective-permute-done | bytes 1048608 | tf_op jit(solution)/shard_map/ppermute | solution.py:33
  79.2 26.5 %all-to-all-done.2 = bf16[8,128,1280]{2,1,0:T(8,128)(2,1)} async-done(((bf16[8,128,1280]{2,1,0:T(8,128)(2,1)}), bf16[8,128,1280]{2,1,0:T(8,128)(2,1)}, u32[]{:S(2)}, u32[]{:S(2)}) %all-to-all-start.2) | async-done | bytes 2621472 | tf_op jit(solution)/shard_map/all_to_all | solution.py:262
  105.7 4.8 %convolution_convert_fusion = bf16[1024,1280]{1,0:T(8,128)(2,1)S(1)} fusion(bf16[1024,1024]{1,0:T(8,128)(2,1)S(1)} %bitcast.71, bf16[1024,1280]{1,0:T(8,128)(2,1)} %bitcast.6), kind=kOutput, calls=%fused_computation | convolution fusion | flops 2685665280 | bytes 7340032 | tf_op jit(solution)/shard_map/dot_general | solution.py:271
  110.5 37.4 %all_to_all.36 = bf16[16,64,1280]{2,1,0:T(8,128)(2,1)S(1)} all-to-all(bf16[16,64,1280]{2,1,0:T(8,128)(2,1)S(1)} %bitcast.70), channel_id=1, replica_groups=mesh['y'=4,'x'=4,'z'=4,'c'=2] {'y','x'}, dimensions={0} | all-to-all | bytes 5242880 | tf_op jit(solution)/shard_map/all_to_all | solution.py:272
  149.0 5.3 %all-to-all-start.4 = ((bf16[8,8,1280]{2,1,0:T(8,128)(2,1)}), bf16[8,8,1280]{2,1,0:T(8,128)(2,1)S(1)}, u32[]{:S(2)}, u32[]{:S(2)}) async-start(bf16[8,8,1280]{2,1,0:T(8,128)(2,1)} %bitcast.8), calls=%async_computation.4 | async-start | bytes 327680 | tf_op jit(solution)/shard_map/all_to_all | solution.py:274
  155.0 4.9 %all-to-all-done.4 = bf16[8,8,1280]{2,1,0:T(8,128)(2,1)S(1)} async-done(((bf16[8,8,1280]{2,1,0:T(8,128)(2,1)}), bf16[8,8,1280]{2,1,0:T(8,128)(2,1)S(1)}, u32[]{:S(2)}, u32[]{:S(2)}) %all-to-all-start.4) | async-done | bytes 163872 | tf_op jit(solution)/shard_map/all_to_all | solution.py:274
  161.9 18.6 %attend.1 = bf16[4,8,16,128]{3,2,1,0:T(8,128)(2,1)} custom-call(s32[24]{0:T(128)} %reshape.103.table_ref, s32[4]{0:T(128)} %length_ref.3, bf16[4,8,16,128]{3,2,1,0:T(8,128)(2,1)} %bitcast.76, bf16[4,2,1024]{2,1,0:T(2,128)(2,1)} %copy.36.k_ref, bf16[4,2,1024]{2,1,0:T(2,128)(2,1)} %copy.37.v_ref, bf16[24,128,2048]{2,1,0:T(8,128)(2,1)} %bitcast.61, ...), custom_call_target="tpu_custom_call" | custom-call | flops 200000000 | bytes 13000000 | tf_op jit(solution)/shard_map/attend/pallas_call | solution.py:159
  186.1 4.4 %moved_blocks.1 = bf16[3,128,2048]{2,1,0:T(8,128)(2,1)} custom-call(s32[3]{0:T(128)} %pad_add_fusion.want_ref, s32[24]{0:T(128)} %reshape.103.table_ref, s32[4]{0:T(128)} %length_ref.3, bf16[8,2048]{1,0:T(8,128)(2,1)} %bitcast.77, bf16[24,128,2048]{2,1,0:T(8,128)(2,1)} %bitcast.67), custom_call_target="tpu_custom_call" | custom-call | flops 1000000 | bytes 3200000 | tf_op jit(solution)/shard_map/moved_blocks/pallas_call | solution.py:198
  198.0 10.9 %collective-permute-done.1 = bf16[128,2048]{1,0:T(8,128)(2,1)} collective-permute-done((bf16[128,2048]{1,0:T(8,128)(2,1)S(1)}, bf16[128,2048]{1,0:T(8,128)(2,1)}, u32[]{:S(2)}, u32[]{:S(2)}) %collective-permute-start.1) | collective-permute-done | bytes 524320 | tf_op jit(solution)/shard_map/ppermute | solution.py:29
  210.2 14.8 %all-gather.3.cloned.1.call-done = bf16[256,8192]{1,0:T(8,128)(2,1)} async-done(((bf16[8,8192]{1,0:T(8,128)(2,1)}), bf16[256,8192]{1,0:T(8,128)(2,1)}) %all-gather.3.cloned.1.call-update) | async-done | bytes 4194320 | tf_op jit(solution)/shard_map/all_gather | solution.py:290
  225.1 7.7 %fusion = bf16[32,8,512]{2,1,0:T(8,128)(2,1)} fusion(bf16[256,8192]{1,0:T(8,128)(2,1)} %all-gather.3.cloned.1.call-done, bf16[512,8192]{1,0:T(8,128)(2,1)} %bitcast.80), kind=kOutput, calls=%fused_computation.3 | convolution fusion | flops 2147614720 | bytes 12845056 | tf_op jit(solution)/shard_map/dot_general | solution.py:291
  232.8 5.3 %all-to-all-start.5 = ((bf16[32,8,512]{2,1,0:T(8,128)(2,1)}), bf16[32,8,512]{2,1,0:T(8,128)(2,1)S(1)}, u32[]{:S(2)}, u32[]{:S(2)}) async-start(bf16[32,8,512]{2,1,0:T(8,128)(2,1)} %fusion), calls=%async_computation.5 | async-start | bytes 524288 | tf_op jit(solution)/shard_map/all_to_all | solution.py:293
  238.1 8.9 %all-to-all-done.5.in_ref = bf16[32,8,512]{2,1,0:T(8,128)(2,1)S(1)} async-done(((bf16[32,8,512]{2,1,0:T(8,128)(2,1)}), bf16[32,8,512]{2,1,0:T(8,128)(2,1)S(1)}, u32[]{:S(2)}, u32[]{:S(2)}) %all-to-all-start.5) | async-done | bytes 262176 | tf_op jit(solution)/shard_map/all_to_all | solution.py:293
  247.8 4.8 %panel_order.1 = bf16[32,8,256]{2,1,0:T(8,128)(2,1)} custom-call(s32[128]{0:T(128)} %get-tuple-element.15.from_ref, s32[128]{0:T(128)} %get-tuple-element.14.at_ref, s32[128]{0:T(128)} %get-tuple-element.13.half_ref, bf16[32,8,512]{2,1,0:T(8,128)(2,1)} %copy-done.2), custom_call_target="tpu_custom_call" | custom-call | tf_op jit(solution)/shard_map/panel_order/pallas_call | solution.py:235
  252.5 3.7 %all-to-all-start.6 = ((bf16[32,8,256]{2,1,0:T(8,128)(2,1)}), bf16[32,8,256]{2,1,0:T(8,128)(2,1)S(1)}, u32[]{:S(2)}, u32[]{:S(2)}) async-start(bf16[32,8,256]{2,1,0:T(8,128)(2,1)} %panel_order.1), calls=%async_computation.6 | async-start | bytes 262144 | tf_op jit(solution)/shard_map/all_to_all | solution.py:297
  256.3 7.7 %all-to-all-done.6 = bf16[32,8,256]{2,1,0:T(8,128)(2,1)S(1)} async-done(((bf16[32,8,256]{2,1,0:T(8,128)(2,1)}), bf16[32,8,256]{2,1,0:T(8,128)(2,1)S(1)}, u32[]{:S(2)}, u32[]{:S(2)}) %all-to-all-start.6) | async-done | bytes 131104 | tf_op jit(solution)/shard_map/all_to_all | solution.py:297
  (59 shorter events, 25.0 us)
Async XLA Ops:
  7.2 203.0 %all-gather.5.cloned.1.call-start = ((), (), s32[]{:S(2)}) async-start(), calls=%async_computation.8 | async-start | bytes 10485760 | tf_op jit(solution)/shard_map/all_gather | solution.py:255
  10.3 0.7 copy-start.5
  11.6 20.8 %all-to-all-start = ((s32[128,1,2]{2,1,0:T(1,128)}), s32[128,1,2]{2,1,0:T(1,128)S(1)}, u32[]{:S(2)}, u32[]{:S(2)}) async-start(s32[128,1,2]{2,1,0:T(1,128)} %broadcast_in_dim.34), calls=%async_computation | async-start | bytes 131072 | tf_op jit(solution)/shard_map/all_to_all | solution.py:257
  37.6 28.0 %all-to-all-start.1 = ((bf16[16,32,1024]{2,1,0:T(8,128)(2,1)}), bf16[16,32,1024]{2,1,0:T(8,128)(2,1)S(1)}, u32[]{:S(2)}, u32[]{:S(2)}) async-start(bf16[16,32,1024]{2,1,0:T(8,128)(2,1)} %bitcast.69), calls=%async_computation.1 | async-start | bytes 2097152 | tf_op jit(solution)/shard_map/all_to_all | solution.py:266
  65.5 40.2 %all-to-all-start.2 = ((bf16[8,128,1280]{2,1,0:T(8,128)(2,1)}), bf16[8,128,1280]{2,1,0:T(8,128)(2,1)}, u32[]{:S(2)}, u32[]{:S(2)}) async-start(bf16[8,128,1280]{2,1,0:T(8,128)(2,1)} %split_heads.1), calls=%async_computation.2 | async-start | bytes 5242880 | tf_op jit(solution)/shard_map/all_to_all | solution.py:262
  73.7 2.8 %collective-permute-start = (bf16[16,32,1024]{2,1,0:T(8,128)(2,1)S(1)}, bf16[16,32,1024]{2,1,0:T(8,128)(2,1)S(1)}, u32[]{:S(2)}, u32[]{:S(2)}) collective-permute-start(bf16[16,32,1024]{2,1,0:T(8,128)(2,1)S(1)} %all-to-all-done.1), channel_id=1, source_target_pairs={{0,1},{1,0},{2,3},{3,2},{4,5},{5,4},{6,7},{7,6},{8,9},{9,8},{10,11... | collective-permute-start | bytes 3145736 | tf_op jit(solution)/shard_map/ppermute | solution.py:33
  76.4 1.0 copy-start.1
  148.0 6.4 %copy-start.4 = (s32[4,6]{1,0:T(4,128)S(1)}, s32[4,6]{1,0:T(4,128)}, u32[]{:S(2)}) copy-start(s32[4,6]{1,0:T(4,128)} %param.15) | copy-start | bytes 292
  149.0 10.9 %all-to-all-start.4 = ((bf16[8,8,1280]{2,1,0:T(8,128)(2,1)}), bf16[8,8,1280]{2,1,0:T(8,128)(2,1)S(1)}, u32[]{:S(2)}, u32[]{:S(2)}) async-start(bf16[8,8,1280]{2,1,0:T(8,128)(2,1)} %bitcast.8), calls=%async_computation.4 | async-start | bytes 327680 | tf_op jit(solution)/shard_map/all_to_all | solution.py:274
  154.3 70.7 %all-gather.3.cloned.1.call-start = ((), (), s32[]{:S(2)}) async-start(), calls=%async_computation.7 | async-start | bytes 4325376 | tf_op jit(solution)/shard_map/all_gather | solution.py:290
  161.9 20.4 %copy-start.3 = (s32[1,1,4,1]{2,3,1,0:T(1,128)S(1)}, s32[1,1,4,1]{2,3,1,0:T(1,128)}, u32[]{:S(2)}) copy-start(s32[1,1,4,1]{2,3,1,0:T(1,128)} %param.17) | copy-start | bytes 52
  193.0 15.8 %collective-permute-start.1 = (bf16[128,2048]{1,0:T(8,128)(2,1)S(1)}, bf16[128,2048]{1,0:T(8,128)(2,1)}, u32[]{:S(2)}, u32[]{:S(2)}) collective-permute-start(bf16[128,2048]{1,0:T(8,128)(2,1)S(1)} %get-tuple-element.5), channel_id=1, source_target_pairs={{0,32},{32,64},{64,96},{96,0},{1,33},{33,65},{65,97},{97,1},{2,34}... | collective-permute-start | bytes 1572872 | tf_op jit(solution)/shard_map/ppermute | solution.py:29
  195.1 42.9 %collective-permute-start.2 = (bf16[128,2048]{1,0:T(8,128)(2,1)}, bf16[128,2048]{1,0:T(8,128)(2,1)S(1)}, u32[]{:S(2)}, u32[]{:S(2)}) collective-permute-start(bf16[128,2048]{1,0:T(8,128)(2,1)} %get-tuple-element.4), channel_id=1, source_target_pairs={{0,64},{32,96},{64,0},{96,32},{1,65},{33,97},{65,1},{97,33},{2,66}... | collective-permute-start | bytes 1572872 | tf_op jit(solution)/shard_map/ppermute | solution.py:29
  196.3 59.9 %collective-permute-start.3 = (bf16[128,2048]{1,0:T(8,128)(2,1)}, bf16[128,2048]{1,0:T(8,128)(2,1)S(1)}, u32[]{:S(2)}, u32[]{:S(2)}) collective-permute-start(bf16[128,2048]{1,0:T(8,128)(2,1)} %get-tuple-element.3), channel_id=1, source_target_pairs={{0,96},{32,0},{64,32},{96,64},{1,97},{33,1},{65,33},{97,65},{2,98}... | collective-permute-start | bytes 1572872 | tf_op jit(solution)/shard_map/ppermute | solution.py:29
  232.8 14.3 %all-to-all-start.5 = ((bf16[32,8,512]{2,1,0:T(8,128)(2,1)}), bf16[32,8,512]{2,1,0:T(8,128)(2,1)S(1)}, u32[]{:S(2)}, u32[]{:S(2)}) async-start(bf16[32,8,512]{2,1,0:T(8,128)(2,1)} %fusion), calls=%async_computation.5 | async-start | bytes 524288 | tf_op jit(solution)/shard_map/all_to_all | solution.py:293
  247.1 0.7 copy-start.2
  252.5 11.5 %all-to-all-start.6 = ((bf16[32,8,256]{2,1,0:T(8,128)(2,1)}), bf16[32,8,256]{2,1,0:T(8,128)(2,1)S(1)}, u32[]{:S(2)}, u32[]{:S(2)}) async-start(bf16[32,8,256]{2,1,0:T(8,128)(2,1)} %panel_order.1), calls=%async_computation.6 | async-start | bytes 262144 | tf_op jit(solution)/shard_map/all_to_all | solution.py:297
  256.3 9.1 %copy-start = (bf16[1,4,128,2048]{3,2,1,0:T(8,128)(2,1)}, bf16[1,4,128,2048]{3,2,1,0:T(8,128)(2,1)S(1)}, u32[]{:S(2)}) copy-start(bf16[1,4,128,2048]{3,2,1,0:T(8,128)(2,1)S(1)} %bitcast_dynamic-update-slice_fusion) | copy-start | bytes 6291460
Sparse Core Ops, SparseCore 0:
  10.5 97.8 all-gather.4
  182.4 42.6 all-gather.2
where the time goes:
time: 273 us; the launch traced here: 272 us
  waiting for transfers between devices  104 us (38%)
  starting transfers between devices  40.5 us (15%)
  Pallas kernels  38.1 us (14%)
  blocking collectives  37.4 us (14%)
  local copies, waits for them, and re-layouts  18.3 us (7%)
  between operations  14.3 us (5%)
  matrix products  12.5 us (5%)
  other arithmetic  6.89 us (3%)
    all_to_all x1, blocking collectives, per_device(): lax.all_to_all(partial.reshape(16, 64, GROUP), ('y', 'x'), 0, 0, tiled=True)  37.4 us
    all_to_all x1, waiting for transfers between devices, per_device(): lax.all_to_all(split_heads(panels), ('z', 'c'), 0, 0, tiled=True)  26.5 us
    pallas_call x1, Pallas kernels, attend(): pl.pallas_call(attend_kernel, grid_spec=pltpu.PrefetchScalarGridSpec(num_...  18.6 us
    all_to_all x1, waiting for transfers between devices, per_device(): lax.all_to_all(picked.reshape(16, 32, 1024), ('y', 'z'), 0, 0, tiled=True)  18.3 us
    all_gather x1, waiting for transfers between devices, per_device(): mixed = lax.all_gather(mixed, plane, axis=0, tiled=True)  14.8 us
    all_to_all x1, starting transfers between devices, per_device(): lax.all_to_all(jnp.broadcast_to(panel_ids[None], (128, 2)), ('y', 'x', 'z...  11.5 us
    ppermute x3, waiting for transfers between devices, shift(): return lax.ppermute(v, axis, [(i, (i + k) % 4) for i in range(4)])  10.9 us
    all_to_all x1, waiting for transfers between devices, per_device(): lax.all_to_all(jnp.broadcast_to(panel_ids[None], (128, 2)), ('y', 'x', 'z...  9.32 us
  transfers between devices with their start and end apart: 12, of which 9 were waited for; matrix products, arithmetic and copies ran while one was open for 11% of the time, Pallas kernels for 14%

commit v1 on v0

--- a/solution.py
+++ b/solution.py
@@ -22,6 +22,7 @@
 BF = jnp.bfloat16
 F32 = jnp.float32
 ROWS = 16
+FIRST, LAST = (0, 2, 3, 4, 6, 7), (1, 2, 3, 5, 6, 7)
 VMEM = 60 * 2**20
 
 
@@ -33,28 +34,120 @@
     return lax.ppermute(v, "c", [(0, 1), (1, 0)])
 
 
-def split_kernel(q_ref, k_ref, v_ref, out_ref):
-    for s in range(2):
-        rows = slice(s * PR, (s + 1) * PR)
-        out_ref[0, rows, :1024] = q_ref[s]
-        out_ref[0, rows, 1024 : 1024 + HD] = k_ref[s]
-        out_ref[0, rows, 1024 + HD :] = v_ref[s]
-
-
-def split_heads(panels):
+def split_kernel(place_ref, q_ref, k_ref, v_ref, *outs):
+    step = pl.program_id(0)
+    for out_ref, first, last in zip(outs, FIRST, LAST):
+
+        @pl.when(jnp.logical_and(step >= first, step <= last))
+        def _(out_ref=out_ref):
+            for s in range(2):
+                rows = slice(s * PR, (s + 1) * PR)
+                out_ref[0, rows, :1024] = q_ref[s]
+                out_ref[0, rows, 1024 : 1024 + HD] = k_ref[s]
+                out_ref[0, rows, 1024 + HD :] = v_ref[s]
+
+
+def split_heads(place, panels):
+    def group(k, p):
+        core = jnp.where(jnp.logical_or(k == 3, jnp.logical_or(k == 1, jnp.logical_or(k == 5, k == 7))), 1, 0)
+        return lax.rem(p[0] + k // 2 + 1, 4) * 2 + lax.rem(p[1] + core, 2)
+
+    def piece(first, last):
+        return pl.BlockSpec(
+            (1, 2 * PR, GROUP), lambda k, p: (jnp.clip(k, first, last) - first, 0, 0)
+        )
+
     return pl.pallas_call(
         split_kernel,
-        grid=(KVH,),
-        in_specs=[
-            pl.BlockSpec((2, PR, 1024), lambda g: (0, 0, g)),
-            pl.BlockSpec((2, PR, HD), lambda g: (0, 0, D // HD + g)),
-            pl.BlockSpec((2, PR, HD), lambda g: (0, 0, (D + KV) // HD + g)),
-        ],
-        out_specs=pl.BlockSpec((1, 2 * PR, GROUP), lambda g: (g, 0, 0)),
-        out_shape=jax.ShapeDtypeStruct((KVH, 2 * PR, GROUP), BF),
+        grid_spec=pltpu.PrefetchScalarGridSpec(
+            num_scalar_prefetch=1,
+            grid=(8,),
+            in_specs=[
+                pl.BlockSpec((2, PR, 1024), lambda k, p: (0, 0, group(k, p))),
+                pl.BlockSpec((2, PR, HD), lambda k, p: (0, 0, D // HD + group(k, p))),
+                pl.BlockSpec((2, PR, HD), lambda k, p: (0, 0, (D + KV) // HD + group(k, p))),
+            ],
+            out_specs=[piece(a, b) for a, b in zip(FIRST, LAST)],
+        ),
+        out_shape=[jax.ShapeDtypeStruct((n, 2 * PR, GROUP), BF) for n in (2, 1, 1, 2, 1, 1)],
         cost_estimate=pl.CostEstimate(flops=0, bytes_accessed=5_300_000, transcendentals=0),
         name="split_heads",
-    )(panels, panels, panels)
+    )(place, panels, panels, panels)
+
+
+def project_kernel(core_ref, mine_ref, other_ref, *refs):
+    pieces, (out_ref, w_ref) = refs[:8], refs[8:]
+    core = core_ref[0]
+
+    @pl.when(pl.program_id(0) == 0)
+    def _():
+        for i, piece in enumerate(pieces):
+            slot = jnp.where(i % 2 == 0, core, 1 - core)
+            at = pl.multiple_of((i // 2) * 256 + slot * 128, 128)
+            w_ref[pl.ds(at, 128), :] = piece[0]
+
+    mine, other = mine_ref[...], other_ref[...]
+    low = core == 0
+    x = jnp.concatenate([jnp.where(low, mine, other), jnp.where(low, other, mine)], axis=1)
+    x = x.reshape(256, 1024)
+    for lo in range(0, GROUP, 256):
+        total = jnp.dot(x, w_ref[:, lo : lo + 256], preferred_element_type=F32)
+        out_ref[:, :, lo : lo + 256] = total.reshape(4, 64, 256).astype(BF)
+
+
+def project(core, mine, other, *pieces):
+    rows = pl.BlockSpec((4, 32, 1024), lambda i, c: (i, 0, 0))
+    return pl.pallas_call(
+        project_kernel,
+        grid_spec=pltpu.PrefetchScalarGridSpec(
+            num_scalar_prefetch=1,
+            grid=(4,),
+            in_specs=[
+                rows,
+                rows,
+                *[pl.BlockSpec((1, 2 * PR, GROUP), lambda i, c, at=at: (at, 0, 0)) for _, at in pieces],
+            ],
+            out_specs=pl.BlockSpec((4, 64, GROUP), lambda i, c: (i, 0, 0)),
+            scratch_shapes=[pltpu.VMEM((16 * PR, GROUP), BF)],
+        ),
+        out_shape=jax.ShapeDtypeStruct((16, 64, GROUP), BF),
+        compiler_params=pltpu.CompilerParams(vmem_limit_bytes=VMEM),
+        cost_estimate=pl.CostEstimate(flops=2_700_000_000, bytes_accessed=7_500_000, transcendentals=0),
+        name="project",
+    )(core, mine, other, *[v for v, _ in pieces])
+
+
+def output_kernel(x_ref, *refs):
+    pieces, (out_ref, sum_ref) = refs[:8], refs[8:]
+    k = pl.program_id(0)
+
+    @pl.when(k == 0)
+    def _():
+        sum_ref[...] = jnp.zeros_like(sum_ref)
+
+    w = jnp.concatenate([r[0] for r in pieces], axis=0)
+    sum_ref[...] += lax.dot_general(x_ref[...], w, (((1,), (1,)), ((), ())), preferred_element_type=F32)
+
+    @pl.when(k == pl.num_programs(0) - 1)
+    def _():
+        out_ref[...] = sum_ref[...].reshape(32, 8, 512).astype(BF)
+
+
+def output_product(x, w):
+    return pl.pallas_call(
+        output_kernel,
+        grid=(4,),
+        in_specs=[
+            pl.BlockSpec((256, 2048), lambda k: (0, k)),
+            *[pl.BlockSpec((1, PR, 2048), lambda k, i=i: (i, 0, k)) for i in range(8)],
+        ],
+        out_specs=pl.BlockSpec((32, 8, 512), lambda k: (0, 0, 0)),
+        out_shape=jax.ShapeDtypeStruct((32, 8, 512), BF),
+        scratch_shapes=[pltpu.VMEM((256, 512), F32)],
+        compiler_params=pltpu.CompilerParams(vmem_limit_bytes=VMEM),
+        cost_estimate=pl.CostEstimate(flops=2_150_000_000, bytes_accessed=12_800_000, transcendentals=0),
+        name="output_product",
+    )(x, *[w] * 8)
 
 
 def pick_kernel(ids_ref, at_ref, first_ref, second_ref, gain_ref, out_ref, x_ref, scale_ref):
@@ -90,7 +183,8 @@
         both = jnp.where(lane < 64, a, b).astype(BF)
         both = jnp.dot(turn, both, preferred_element_type=F32).astype(BF)
         for z in range(4):
-            out_ref[0, z, :, pair * 128 : (pair + 1) * 128] = both
+            at = (pair // 2 - z) % 4 * 256 + pair % 2 * 128
+            out_ref[0, z, :, at : at + 128] = both
 
 
 def pick_columns(ids, at, first, second, gain):
@@ -114,27 +208,38 @@
 
 
 def attend_kernel(table_ref, length_ref, q_ref, k_ref, v_ref, *refs):
-    blocks, out_ref = refs[:MAXB], refs[MAXB]
+    blocks, (out_ref, score_ref, prob_ref, sum_ref) = refs[:MAXB], refs[MAXB:]
     r = pl.program_id(0)
     length = length_ref[r]
     inverse_root = 1.0 / math.sqrt(HD)
+    lane = lax.broadcasted_iota(jnp.int32, (16, 128), 1)
     row = lax.broadcasted_iota(jnp.int32, (16, 128), 0)
-    lane = lax.broadcasted_iota(jnp.int32, (16, 128), 1)
     fresh_seen = jnp.logical_or(lane == 0, jnp.logical_and(lane == 1, row >= 8))
     nt = (((1,), (1,)), ((), ()))
     pad = jnp.zeros((126, HD), F32)
+
+    for b in range(MAXB):
+        seen = b * BLK < length
+
+        @pl.when(seen)
+        def _(b=b):
+            for g in range(KVH):
+                keys = blocks[b][0, :, 2 * g * HD : (2 * g + 1) * HD]
+                s = lax.dot_general(q_ref[0, g], keys, nt, preferred_element_type=F32) * inverse_root
+                score_ref[b, g * 16 : (g + 1) * 16] = jnp.where(lane + b * BLK < length, s, -1e30)
+
+        @pl.when(jnp.logical_not(seen))
+        def _(b=b):
+            score_ref[b] = jnp.full((128, 128), -1e30, F32)
+
     for g in range(KVH):
-        lo = g * HD
-        q = q_ref[0, g]
-        new_k = jnp.concatenate([k_ref[0, :, lo : lo + HD].astype(F32), pad], axis=0).astype(BF)
-        new_v = jnp.concatenate([v_ref[0, :, lo : lo + HD].astype(F32), pad], axis=0).astype(BF)
-        scores = []
-        for b in range(MAXB):
-            keys = blocks[b][0, :, 2 * lo : 2 * lo + HD]
-            s = lax.dot_general(q, keys, nt, preferred_element_type=F32) * inverse_root
-            scores.append(jnp.where(lane + b * BLK < length, s, -1e30))
-        s = lax.dot_general(q, new_k, nt, preferred_element_type=F32) * inverse_root
-        scores.append(jnp.where(fresh_seen, s, -1e30))
+        new_k = jnp.concatenate([k_ref[0, :, g * HD : (g + 1) * HD].astype(F32), pad], axis=0)
+        s = lax.dot_general(q_ref[0, g], new_k.astype(BF), nt, preferred_element_type=F32) * inverse_root
+        score_ref[MAXB, g * 16 : (g + 1) * 16] = jnp.where(fresh_seen, s, -1e30)
+
+    for g in range(KVH):
+        rows = slice(g * 16, (g + 1) * 16)
+        scores = [score_ref[b, rows] for b in range(MAXB + 1)]
         top = scores[0]
         for s in scores[1:]:
             top = jnp.maximum(top, s)
@@ -143,13 +248,25 @@
         total = weights[0]
         for p in weights[1:]:
             total = total + p
-        total = jnp.sum(total, axis=1, keepdims=True)
-        inverse = 1.0 / total
-        mixed = jnp.dot((weights[MAXB] * inverse).astype(BF), new_v, preferred_element_type=F32)
-        for b in range(MAXB):
-            vals = blocks[b][0, :, 2 * lo + HD : 2 * lo + 2 * HD]
-            mixed += jnp.dot((weights[b] * inverse).astype(BF), vals, preferred_element_type=F32)
-        out_ref[0, g] = mixed.astype(BF)
+        inverse = 1.0 / jnp.sum(total, axis=1, keepdims=True)
+        for b in range(MAXB + 1):
+            prob_ref[b, rows] = (weights[b] * inverse).astype(BF)
+
+    for g in range(KVH):
+        rows = slice(g * 16, (g + 1) * 16)
+        new_v = jnp.concatenate([v_ref[0, :, g * HD : (g + 1) * HD].astype(F32), pad], axis=0)
+        sum_ref[rows] = jnp.dot(prob_ref[MAXB, rows], new_v.astype(BF), preferred_element_type=F32)
+
+    for b in range(MAXB):
+
+        @pl.when(b * BLK < length)
+        def _(b=b):
+            for g in range(KVH):
+                rows = slice(g * 16, (g + 1) * 16)
+                vals = blocks[b][0, :, (2 * g + 1) * HD : (2 * g + 2) * HD]
+                sum_ref[rows] += jnp.dot(prob_ref[b, rows], vals, preferred_element_type=F32)
+
+    out_ref[0] = sum_ref[...].reshape(KVH, 16, HD).astype(BF)
 
 
 def attend(table, length, q, k, v, cache):
@@ -168,6 +285,11 @@
                 *[block(b) for b in range(MAXB)],
             ],
             out_specs=pl.BlockSpec((1, KVH, 16, HD), lambda r, t, n: (r, 0, 0, 0)),
+            scratch_shapes=[
+                pltpu.VMEM((MAXB + 1, 128, 128), F32),
+                pltpu.VMEM((MAXB + 1, 128, 128), BF),
+                pltpu.VMEM((128, HD), F32),
+            ],
         ),
         out_shape=jax.ShapeDtypeStruct((4, KVH, 16, HD), BF),
         compiler_params=pltpu.CompilerParams(vmem_limit_bytes=VMEM),
@@ -228,7 +350,7 @@
             out_ref[q, :, s * 128 : (s + 1) * 128] = both.astype(BF)
         return 0
 
-    lax.fori_loop(0, 32, step, 0)
+    lax.fori_loop(0, 32, step, 0, unroll=4)
 
 
 def panel_order(source, at, half, arrived):
@@ -252,24 +374,46 @@
     table = block_table.reshape(-1)
     plane = ("x", "z", "c")
 
-    w_o = lax.all_gather(panels[:, :, QKV:], "y", axis=0, tiled=True).reshape(8 * PR, D)
-
-    ids = lax.all_to_all(
-        jnp.broadcast_to(panel_ids[None], (128, 2)), ("y", "x", "z", "c"), 0, 0, tiled=True
+    right, far_a, far_b, left, own_a, own_b = split_heads(jnp.stack([z, c]), panels)
+    own_b = swap(own_b)
+
+    near = lax.all_to_all(
+        jnp.broadcast_to(panel_ids, (32, 8, 64, 2)).reshape(32, 8, 128), ("y", "z", "c"), 0, 0, tiled=True
+    )[:, 0, :2].reshape(64)
+    near, right, left, far_a, far_b, w_o = lax.optimization_barrier(
+        (near, right, left, far_a, far_b, panels[:, :, QKV:])
     )
-    near = lax.dynamic_index_in_dim(ids.reshape(4, 4, 16), x, 1, keepdims=False).reshape(64)
-
-    w_in = lax.all_to_all(split_heads(panels), ("z", "c"), 0, 0, tiled=True).reshape(16 * PR, GROUP)
+    w_o = lax.all_gather(w_o, "y", axis=0, tiled=True)
+    far_a = shift(far_a, "z", 1)
+    far_b = shift(far_b, "z", -1)
+    from_left = shift(right, "z", 1)
+    from_right = shift(left, "z", -1)
 
     block = (z * 2 + c).reshape(1)
-    picked = pick_columns(near, block, first, second, gain.reshape(1, D))
-    rows = lax.all_to_all(picked.reshape(16, 32, 1024), ("y", "z"), 0, 0, tiled=True)
-    other = swap(rows)
-    rows = jnp.where(
-        c == 0, jnp.stack([rows, other], axis=1), jnp.stack([other, rows], axis=1)
-    ).reshape(64 * ROWS, 1024)
-    partial = jnp.dot(rows, w_in, preferred_element_type=F32).astype(BF)
-    parts = lax.all_to_all(partial.reshape(16, 64, GROUP), ("y", "x"), 0, 0, tiled=True)
+    picked = pick_columns(near, block, first, second, gain.reshape(1, D)).reshape(16, 32, 1024)
+    picked, far_a, far_b = lax.optimization_barrier((picked, far_a, far_b))
+    far_a = shift(far_a, "z", 1)
+    far_b = shift(far_b, "z", -1)
+    rows = lax.all_to_all(picked, ("y", "z"), 0, 0, tiled=True)
+    rows, from_left, from_right, far_a, far_b = lax.optimization_barrier(
+        (rows, from_left, from_right, far_a, far_b)
+    )
+    left_b = swap(from_left[1:])
+    right_b = swap(from_right[1:])
+    partial = project(
+        c.reshape(1),
+        rows,
+        swap(rows),
+        (own_a, 0),
+        (own_b, 0),
+        (from_right, 0),
+        (right_b, 0),
+        (far_a, 0),
+        (swap(far_b), 0),
+        (from_left, 0),
+        (left_b, 0),
+    )
+    parts = lax.all_to_all(partial, ("y", "x"), 0, 0, tiled=True)
     summed = jnp.sum(parts.astype(F32), axis=0).astype(BF)
     projected = lax.all_to_all(summed.reshape(8, 8, GROUP), ("z", "c"), 0, 0, tiled=True)
     projected = projected.reshape(KVH, 2, 4, GROUP)
@@ -284,16 +428,19 @@
     want = jnp.stack([lax.dynamic_index_in_dim(want, (y + k) % 4, 0, keepdims=False) for k in (1, 2, 3)])
     moving = moved_blocks(want, table, lengths, fresh, cache)
     got = [shift(moving[k - 1], "y", k) for k in (1, 2, 3)]
-
     mixed = attend(table, lengths, query, new_k, new_v, cache)
     mixed = mixed.reshape(4, KVH, 2, 8, HD).transpose(2, 0, 1, 3, 4).reshape(8, D)
+    mixed, near = lax.optimization_barrier((mixed, near))
     mixed = lax.all_gather(mixed, plane, axis=0, tiled=True)
-    out = lax.dot_general(mixed, w_o, (((1,), (1,)), ((), ())), preferred_element_type=F32)
-
-    arrived = lax.all_to_all(out.astype(BF).reshape(32, 8, 512), plane, 0, 0, tiled=True)
+    out = output_product(mixed, w_o)
+
+    ids = lax.all_to_all(jnp.broadcast_to(near[None], (4, 64)), "x", 0, 0, tiled=True)
     match = ids.reshape(1, 256) == jnp.arange(PANELS, dtype=jnp.int32)[:, None]
     slot = jnp.sum(jnp.where(match, jnp.arange(256, dtype=jnp.int32)[None, :], 0), axis=1)
-    ordered = panel_order((slot // 2) % 32, slot // 64, slot % 2, arrived)
+    source = slot // 64 * 8 + slot // 2 % 8
+    arrived = lax.all_to_all(out, plane, 0, 0, tiled=True)
+    arrived, *got = lax.optimization_barrier((arrived, *got))
+    ordered = panel_order(source, slot // 16 % 4, slot % 2, arrived)
     final = lax.all_to_all(ordered, plane, 0, 0, tiled=True).reshape(32, 2, 4, 256)
 
     hosted = jnp.zeros((4, BLK, 2 * KV), BF)

time: 273 us -> 260 us (0.952)
  waiting for transfers between devices: 104 us -> 81.4 us
  matrix products: 12.5 us -> 0 us
  blocking collectives: 37.4 us -> 45.7 us
  starting transfers between devices: 40.5 us -> 46.8 us
  Pallas kernels: 38.1 us -> 43.7 us
  local copies, waits for them, and re-layouts: 18.3 us -> 21.1 us
    all_to_all x4, waiting for transfers between devices: 63.1 us -> 8.32 us  [the longest x1 8.31 us: per_device(): arrived = lax.all_to_all(out, plane, 0, 0, tiled=True)]
    ppermute x3 -> x9, waiting for transfers between devices: 10.9 us -> 32.6 us  [shift(): return lax.ppermute(v, axis, [(i, (i + k) % 4) for i in range(4)])]
    pallas_call x1 -> x3, Pallas kernels: 5.96 us -> 20.9 us  [the longest x1 7.07 us: output_product(): pl.pallas_call(output_kernel, grid=(4,), in_specs=[pl.BlockSpec((256, 204...]
    dot_general x2 -> x0, matrix products: 12.5 us -> none  [the longest x1 7.73 us: per_device(): lax.dot_general(mixed, w_o, (((1,), (1,)), ((), ())), preferred_element_t...]
    all_gather x1, waiting for transfers between devices: 14.8 us -> 25.9 us  [per_device(): mixed = lax.all_gather(mixed, plane, axis=0, tiled=True)]
    all_to_all x1, blocking collectives: 37.4 us -> 45.7 us  [per_device(): parts = lax.all_to_all(partial, ('y', 'x'), 0, 0, tiled=True)]
    ppermute x3 -> x9, starting transfers between devices: 2.85 us -> 10.8 us  [shift(): return lax.ppermute(v, axis, [(i, (i + k) % 4) for i in range(4)])]
    pallas_call x1, Pallas kernels: 18.6 us -> 10.9 us  [attend(): pl.pallas_call(attend_kernel, grid_spec=pltpu.PrefetchScalarGridSpec(num_...]
  transfers between devices with their start and end apart: 12 -> 22, of which waited for: 9 -> 10; matrix products, arithmetic and copies ran while one was open for 11% -> 7% of each run, Pallas kernels for 14% -> 16%
where the time goes in v1:
time: 260 us; the launch traced here: 259 us
  waiting for transfers between devices  81.4 us (31%)
  starting transfers between devices  46.8 us (18%)
  blocking collectives  45.7 us (18%)
  Pallas kernels  43.7 us (17%)
  local copies, waits for them, and re-layouts  21.1 us (8%)
  between operations  14.3 us (6%)
  other arithmetic  5.51 us (2%)
    all_to_all x1, blocking collectives, per_device(): parts = lax.all_to_all(partial, ('y', 'x'), 0, 0, tiled=True)  45.7 us
    ppermute x9, waiting for transfers between devices, shift(): return lax.ppermute(v, axis, [(i, (i + k) % 4) for i in range(4)])  32.6 us
    all_gather x1, waiting for transfers between devices, per_device(): mixed = lax.all_gather(mixed, plane, axis=0, tiled=True)  25.9 us
    pallas_call x1, Pallas kernels, attend(): pl.pallas_call(attend_kernel, grid_spec=pltpu.PrefetchScalarGridSpec(num_...  10.9 us
    ppermute x9, starting transfers between devices, shift(): return lax.ppermute(v, axis, [(i, (i + k) % 4) for i in range(4)])  10.8 us
    all_to_all x1, starting transfers between devices, per_device(): lax.all_to_all(jnp.broadcast_to(panel_ids, (32, 8, 64, 2)).reshape(32, 8,...  9.6 us
    all_to_all x1, waiting for transfers between devices, per_device(): arrived = lax.all_to_all(out, plane, 0, 0, tiled=True)  8.31 us
    pallas_call x1, Pallas kernels, output_product(): pl.pallas_call(output_kernel, grid=(4,), in_specs=[pl.BlockSpec((256, 204...  7.07 us
  transfers between devices with their start and end apart: 22, of which 10 were waited for; matrix products, arithmetic and copies ran while one was open for 7% of the time, Pallas kernels for 16%

profile of v1, /device:TPU:1, one launch (start us, length us, event | category | flops | bytes accessed | tf_op | source)
XLA Modules:
  0.0 258.5 jit_solution(11156100711512610783)
XLA Ops:
  8.6 9.6 %all-to-all-start = ((s32[32,8,128]{2,1,0:T(8,128)}), s32[32,8,128]{2,1,0:T(8,128)S(1)}, u32[]{:S(2)}, u32[]{:S(2)}) async-start(s32[32,8,128]{2,1,0:T(8,128)} %broadcast_in_dim.43), calls=%async_computation | async-start | bytes 262144 | tf_op jit(solution)/shard_map/all_to_all | solution.py:380
  18.3 3.1 %slice.40 = bf16[2,64,8192]{2,1,0:T(8,128)(2,1)} slice(bf16[2,64,18432]{2,1,0:T(8,128)(2,1)} %v_ref.1), slice={[0:2], [0:64], [10240:18432]} | slice | bytes 4194304 | tf_op jit(solution)/shard_map/slice | solution.py:384
  22.0 7.1 %split_heads.1 = (bf16[2,128,1280]{2,1,0:T(8,128)(2,1)}, bf16[1,128,1280]{2,1,0:T(8,128)(2,1)}, bf16[1,128,1280]{2,1,0:T(8,128)(2,1)}, bf16[2,128,1280]{2,1,0:T(...) custom-call(s32[2]{0:T(128)} %pad_add_fusion.place_ref, bf16[2,64,18432]{2,1,0:T(8,128)(2,1)} %v_ref.1, ...), custom_call_target="tpu_custom_call" | custom-call | bytes 5300000 | tf_op jit(solution)/shard_map/split_heads/pallas_call | solution.py:60
  32.8 4.4 %pick_columns.1 = bf16[4,4,32,1024]{3,2,1,0:T(8,128)(2,1)} custom-call(s32[64]{0:T(128)} %reshape_squeeze.9.ids_ref, s32[1]{0:T(128)} %bitcast.2.at_ref, bf16[128,8192]{1,0:T(8,128)(2,1)} %first_ref.1, bf16[128,8192]{1,0:T(8,128)(2,1)} %second_ref.1, f32[1,8192]{1,0:T(1,128)} %bitcast.63), custom_call_target="tpu_custom_call" | custom-call | flops 20000000 | bytes 2000000 | tf_op jit(solution)/shard_map/pick_columns/pallas_call | solution.py:191
  37.2 3.2 %collective-permute-done = bf16[1,128,1280]{2,1,0:T(8,128)(2,1)S(1)} collective-permute-done((bf16[1,128,1280]{2,1,0:T(8,128)(2,1)S(1)}, bf16[1,128,1280]{2,1,0:T(8,128)(2,1)S(1)}, u32[]{:S(2)}, u32[]{:S(2)}) %collective-permute-start) | collective-permute-done | bytes 327712 | tf_op jit(solution)/shard_map/ppermute | solution.py:30
  41.1 6.2 %all-to-all-start.1 = ((bf16[16,32,1024]{2,1,0:T(8,128)(2,1)}), bf16[16,32,1024]{2,1,0:T(8,128)(2,1)S(1)}, u32[]{:S(2)}, u32[]{:S(2)}) async-start(bf16[16,32,1024]{2,1,0:T(8,128)(2,1)} %bitcast.57), calls=%async_computation.1 | async-start | bytes 2097152 | tf_op jit(solution)/shard_map/all_to_all | solution.py:397
  50.2 2.6 %collective-permute-start.5 = (bf16[1,128,1280]{2,1,0:T(8,128)(2,1)}, bf16[1,128,1280]{2,1,0:T(8,128)(2,1)}, u32[]{:S(2)}, u32[]{:S(2)}) collective-permute-start(bf16[1,128,1280]{2,1,0:T(8,128)(2,1)} %copy-done.13), channel_id=1, source_target_pairs={{0,6},{2,0},{4,2},{6,4},{1,7},{3,1},{5,3},{7,5},{8,14},{10,8},{12,... | collective-permute-start | bytes 983048 | tf_op jit(solution)/shard_map/ppermute | solution.py:30
  52.7 22.4 %collective-permute-done.2.refs_6_ = bf16[2,128,1280]{2,1,0:T(8,128)(2,1)S(1)} collective-permute-done((bf16[2,128,1280]{2,1,0:T(8,128)(2,1)}, bf16[2,128,1280]{2,1,0:T(8,128)(2,1)S(1)}, u32[]{:S(2)}, u32[]{:S(2)}) %collective-permute-start.2) | collective-permute-done | bytes 655392 | tf_op jit(solution)/shard_map/ppermute | solution.py:30
  75.1 7.0 %collective-permute-done.4.refs_4_ = bf16[1,128,1280]{2,1,0:T(8,128)(2,1)S(1)} collective-permute-done((bf16[1,128,1280]{2,1,0:T(8,128)(2,1)S(1)}, bf16[1,128,1280]{2,1,0:T(8,128)(2,1)S(1)}, u32[]{:S(2)}, u32[]{:S(2)}) %collective-permute-start.4) | collective-permute-done | bytes 327712 | tf_op jit(solution)/shard_map/ppermute | solution.py:30
  91.0 6.8 %project.1 = bf16[16,64,1280]{2,1,0:T(8,128)(2,1)} custom-call(s32[1]{0:T(128)} %bitcast.core_ref, bf16[16,32,1024]{2,1,0:T(8,128)(2,1)} %copy-done.1, bf16[16,32,1024]{2,1,0:T(8,128)(2,1)} %copy-done.10, bf16[1,128,1280]{2,1,0:T(8,128)(2,1)} %get-tuple-element.42.refs_0_, bf16[1,128,1280]{2,1,0:T(8,128)(2,1)} %copy-done.14, ...), custom_call_target="tpu_custom_call" | custom-call | flops 2700000000 | bytes 7500000 | tf_op jit(solution)/shard_map/project/pallas_call | solution.py:100
  97.8 45.7 %all_to_all.36 = bf16[16,64,1280]{2,1,0:T(8,128)(2,1)S(1)} all-to-all(bf16[16,64,1280]{2,1,0:T(8,128)(2,1)} %project.1), channel_id=1, replica_groups=mesh['y'=4,'x'=4,'z'=4,'c'=2] {'y','x'}, dimensions={0} | all-to-all | bytes 5242880 | tf_op jit(solution)/shard_map/all_to_all | solution.py:416
  144.5 4.6 %all-to-all-start.3 = ((bf16[8,8,1280]{2,1,0:T(8,128)(2,1)}), bf16[8,8,1280]{2,1,0:T(8,128)(2,1)S(1)}, u32[]{:S(2)}, u32[]{:S(2)}) async-start(bf16[8,8,1280]{2,1,0:T(8,128)(2,1)} %bitcast.5), calls=%async_computation.3 | async-start | bytes 327680 | tf_op jit(solution)/shard_map/all_to_all | solution.py:418
  149.8 4.9 %all-to-all-done.3 = bf16[8,8,1280]{2,1,0:T(8,128)(2,1)S(1)} async-done(((bf16[8,8,1280]{2,1,0:T(8,128)(2,1)}), bf16[8,8,1280]{2,1,0:T(8,128)(2,1)S(1)}, u32[]{:S(2)}, u32[]{:S(2)}) %all-to-all-start.3) | async-done | bytes 163872 | tf_op jit(solution)/shard_map/all_to_all | solution.py:418
  156.7 10.9 %attend.1 = bf16[4,8,16,128]{3,2,1,0:T(8,128)(2,1)} custom-call(s32[24]{0:T(128)} %reshape.75.table_ref, s32[4]{0:T(128)} %length_ref.3, bf16[4,8,16,128]{3,2,1,0:T(8,128)(2,1)} %bitcast.60, bf16[4,2,1024]{2,1,0:T(2,128)(2,1)} %copy.37.k_ref, bf16[4,2,1024]{2,1,0:T(2,128)(2,1)} %copy.38.v_ref, bf16[24,128,2048]{2,1,0:T(8,128)(2,1)} %bitcast.50, ...), custom_call_target="tpu_custom_call" | custom-call | flops 200000000 | bytes 13000000 | tf_op jit(solution)/shard_map/attend/pallas_call | solution.py:276
  169.9 2.5 pad_add_fusion.1.want_ref
  173.0 3.4 %all-to-all-start.4 = ((s32[4,1,64]{2,1,0:T(1,128)}), s32[4,1,64]{2,1,0:T(1,128)S(1)}, u32[]{:S(2)}, u32[]{:S(2)}) async-start(s32[4,1,64]{2,1,0:T(1,128)} %broadcast_in_dim.44), calls=%async_computation.4 | async-start | bytes 4096 | tf_op jit(solution)/shard_map/all_to_all | solution.py:437
  177.1 4.4 %moved_blocks.1 = bf16[3,128,2048]{2,1,0:T(8,128)(2,1)} custom-call(s32[3]{0:T(128)} %pad_add_fusion.1.want_ref, s32[24]{0:T(128)} %reshape.75.table_ref, s32[4]{0:T(128)} %length_ref.3, bf16[8,2048]{1,0:T(8,128)(2,1)} %bitcast.61, bf16[24,128,2048]{2,1,0:T(8,128)(2,1)} %bitcast.56), custom_call_target="tpu_custom_call" | custom-call | flops 1000000 | bytes 3200000 | tf_op jit(solution)/shard_map/moved_blocks/pallas_call | solution.py:320
  187.7 25.9 %all-gather.3.cloned.1.call-done.x_ref = bf16[256,8192]{1,0:T(8,128)(2,1)} async-done(((bf16[8,8192]{1,0:T(8,128)(2,1)}), bf16[256,8192]{1,0:T(8,128)(2,1)}) %all-gather.3.cloned.1.call-update) | async-done | bytes 4194320 | tf_op jit(solution)/shard_map/all_gather | solution.py:434
  213.6 7.1 %output_product.1 = bf16[32,8,512]{2,1,0:T(8,128)(2,1)} custom-call(bf16[256,8192]{1,0:T(8,128)(2,1)} %all-gather.3.cloned.1.call-done.x_ref, bf16[8,64,8192]{2,1,0:T(8,128)(2,1)} %all-gather.5.cloned.1.call-done.refs_0_.refs_1_.refs_2_.refs_3_.refs_4_.refs_5_.refs_6_.refs_7_, ...), custom_call_target="tpu_custom_call" | custom-call | flops 2150000128 | bytes 12800000 | tf_op jit(solution)/shard_map/output_product/pallas_call | solution.py:137
  220.6 5.3 %all-to-all-start.5 = ((bf16[32,8,512]{2,1,0:T(8,128)(2,1)}), bf16[32,8,512]{2,1,0:T(8,128)(2,1)S(1)}, u32[]{:S(2)}, u32[]{:S(2)}) async-start(bf16[32,8,512]{2,1,0:T(8,128)(2,1)} %output_product.1), calls=%async_computation.5 | async-start | bytes 524288 | tf_op jit(solution)/shard_map/all_to_all | solution.py:441
  226.6 8.3 %all-to-all-done.5.in_ref = bf16[32,8,512]{2,1,0:T(8,128)(2,1)S(1)} async-done(((bf16[32,8,512]{2,1,0:T(8,128)(2,1)}), bf16[32,8,512]{2,1,0:T(8,128)(2,1)S(1)}, u32[]{:S(2)}, u32[]{:S(2)}) %all-to-all-start.5) | async-done | bytes 262176 | tf_op jit(solution)/shard_map/all_to_all | solution.py:441
  235.6 3.1 %panel_order.1 = bf16[32,8,256]{2,1,0:T(8,128)(2,1)} custom-call(s32[128]{0:T(128)} %get-tuple-element.66.from_ref, s32[128]{0:T(128)} %get-tuple-element.67.at_ref, s32[128]{0:T(128)} %get-tuple-element.65.half_ref, bf16[32,8,512]{2,1,0:T(8,128)(2,1)} %copy-done.2), custom_call_target="tpu_custom_call" | custom-call | tf_op jit(solution)/shard_map/panel_order/pallas_call | solution.py:357
  238.8 3.7 %all-to-all-start.6 = ((bf16[32,8,256]{2,1,0:T(8,128)(2,1)}), bf16[32,8,256]{2,1,0:T(8,128)(2,1)S(1)}, u32[]{:S(2)}, u32[]{:S(2)}) async-start(bf16[32,8,256]{2,1,0:T(8,128)(2,1)} %panel_order.1), calls=%async_computation.6 | async-start | bytes 262144 | tf_op jit(solution)/shard_map/all_to_all | solution.py:444
  243.6 6.7 %all-to-all-done.6 = bf16[32,8,256]{2,1,0:T(8,128)(2,1)S(1)} async-done(((bf16[32,8,256]{2,1,0:T(8,128)(2,1)}), bf16[32,8,256]{2,1,0:T(8,128)(2,1)S(1)}, u32[]{:S(2)}, u32[]{:S(2)}) %all-to-all-start.6) | async-done | bytes 131104 | tf_op jit(solution)/shard_map/all_to_all | solution.py:444
  (111 shorter events, 35.5 us)
Async XLA Ops:
  8.6 20.5 %all-to-all-start = ((s32[32,8,128]{2,1,0:T(8,128)}), s32[32,8,128]{2,1,0:T(8,128)S(1)}, u32[]{:S(2)}, u32[]{:S(2)}) async-start(s32[32,8,128]{2,1,0:T(8,128)} %broadcast_in_dim.43), calls=%async_computation | async-start | bytes 262144 | tf_op jit(solution)/shard_map/all_to_all | solution.py:380
  18.3 169.4 %all-gather.5.cloned.1.call-start = ((), (), s32[]{:S(2)}) async-start(), calls=%async_computation.8 | async-start | bytes 10485760 | tf_op jit(solution)/shard_map/all_gather | solution.py:386
  30.1 10.3 %collective-permute-start = (bf16[1,128,1280]{2,1,0:T(8,128)(2,1)S(1)}, bf16[1,128,1280]{2,1,0:T(8,128)(2,1)S(1)}, u32[]{:S(2)}, u32[]{:S(2)}) collective-permute-start(bf16[1,128,1280]{2,1,0:T(8,128)(2,1)S(1)} %copy-done.17), channel_id=1, source_target_pairs={{0,2},{2,4},{4,6},{6,0},{1,3},{3,5},{5,7},{7,1},{8,10},{10,12},{12... | collective-permute-start | bytes 983048 | tf_op jit(solution)/shard_map/ppermute | solution.py:30
  31.4 8.9 %collective-permute-start.1 = (bf16[1,128,1280]{2,1,0:T(8,128)(2,1)S(1)}, bf16[1,128,1280]{2,1,0:T(8,128)(2,1)S(1)}, u32[]{:S(2)}, u32[]{:S(2)}) collective-permute-start(bf16[1,128,1280]{2,1,0:T(8,128)(2,1)S(1)} %copy-done.15), channel_id=1, source_target_pairs={{0,6},{2,0},{4,2},{6,4},{1,7},{3,1},{5,3},{7,5},{8,14},{10,8},{12,... | collective-permute-start | bytes 983048 | tf_op jit(solution)/shard_map/ppermute | solution.py:30
  41.1 41.8 %all-to-all-start.1 = ((bf16[16,32,1024]{2,1,0:T(8,128)(2,1)}), bf16[16,32,1024]{2,1,0:T(8,128)(2,1)S(1)}, u32[]{:S(2)}, u32[]{:S(2)}) async-start(bf16[16,32,1024]{2,1,0:T(8,128)(2,1)} %bitcast.57), calls=%async_computation.1 | async-start | bytes 2097152 | tf_op jit(solution)/shard_map/all_to_all | solution.py:397
  47.3 27.8 %collective-permute-start.2 = (bf16[2,128,1280]{2,1,0:T(8,128)(2,1)}, bf16[2,128,1280]{2,1,0:T(8,128)(2,1)S(1)}, u32[]{:S(2)}, u32[]{:S(2)}) collective-permute-start(bf16[2,128,1280]{2,1,0:T(8,128)(2,1)} %get-tuple-element.37), channel_id=1, source_target_pairs={{0,2},{2,4},{4,6},{6,0},{1,3},{3,5},{5,7},{7,1},{8,10},{10,12},{12... | collective-permute-start | bytes 1966088 | tf_op jit(solution)/shard_map/ppermute | solution.py:30
  48.7 26.4 %collective-permute-start.3 = (bf16[2,128,1280]{2,1,0:T(8,128)(2,1)S(1)}, bf16[2,128,1280]{2,1,0:T(8,128)(2,1)S(1)}, u32[]{:S(2)}, u32[]{:S(2)}) collective-permute-start(bf16[2,128,1280]{2,1,0:T(8,128)(2,1)S(1)} %copy-done.11), channel_id=1, source_target_pairs={{0,6},{2,0},{4,2},{6,4},{1,7},{3,1},{5,3},{7,5},{8,14},{10,8},{12,... | collective-permute-start | bytes 1966088 | tf_op jit(solution)/shard_map/ppermute | solution.py:30
  50.1 32.1 %collective-permute-start.4 = (bf16[1,128,1280]{2,1,0:T(8,128)(2,1)S(1)}, bf16[1,128,1280]{2,1,0:T(8,128)(2,1)S(1)}, u32[]{:S(2)}, u32[]{:S(2)}) collective-permute-start(bf16[1,128,1280]{2,1,0:T(8,128)(2,1)S(1)} %collective-permute-done), channel_id=1, source_target_pairs={{0,2},{2,4},{4,6},{6,0},{1,3},{3,5},{5,7},{7,1},{8,10},{10,12},{12... | collective-permute-start | bytes 983048 | tf_op jit(solution)/shard_map/ppermute | solution.py:30
  50.2 32.7 %collective-permute-start.5 = (bf16[1,128,1280]{2,1,0:T(8,128)(2,1)}, bf16[1,128,1280]{2,1,0:T(8,128)(2,1)}, u32[]{:S(2)}, u32[]{:S(2)}) collective-permute-start(bf16[1,128,1280]{2,1,0:T(8,128)(2,1)} %copy-done.13), channel_id=1, source_target_pairs={{0,6},{2,0},{4,2},{6,4},{1,7},{3,1},{5,3},{7,5},{8,14},{10,8},{12,... | collective-permute-start | bytes 983048 | tf_op jit(solution)/shard_map/ppermute | solution.py:30
  75.1 14.8 %copy-start.5 = (bf16[2,128,1280]{2,1,0:T(8,128)(2,1)}, bf16[2,128,1280]{2,1,0:T(8,128)(2,1)S(1)}, u32[]{:S(2)}) copy-start(bf16[2,128,1280]{2,1,0:T(8,128)(2,1)S(1)} %collective-permute-done.2.refs_6_) | copy-start | bytes 1966084
  82.9 6.2 %collective-permute-start.6 = (bf16[16,32,1024]{2,1,0:T(8,128)(2,1)S(1)}, bf16[16,32,1024]{2,1,0:T(8,128)(2,1)S(1)}, u32[]{:S(2)}, u32[]{:S(2)}) collective-permute-start(bf16[16,32,1024]{2,1,0:T(8,128)(2,1)S(1)} %all-to-all-done.1.mine_ref), channel_id=1, source_target_pairs={{0,1},{1,0},{2,3},{3,2},{4,5},{5,4},{6,7},{7,6},{8,9},{9,8},{10,11... | collective-permute-start | bytes 3145736 | tf_op jit(solution)/shard_map/ppermute | solution.py:34
  84.9 3.3 %collective-permute-start.7 = (bf16[1,128,1280]{2,1,0:T(8,128)(2,1)}, bf16[1,128,1280]{2,1,0:T(8,128)(2,1)S(1)}, u32[]{:S(2)}, u32[]{:S(2)}) collective-permute-start(bf16[1,128,1280]{2,1,0:T(8,128)(2,1)} %get-tuple-element.43), channel_id=1, source_target_pairs={{0,1},{1,0},{2,3},{3,2},{4,5},{5,4},{6,7},{7,6},{8,9},{9,8},{10,11... | collective-permute-start | bytes 983048 | tf_op jit(solution)/shard_map/ppermute | solution.py:34
  85.0 3.6 %collective-permute-start.8 = (bf16[1,128,1280]{2,1,0:T(8,128)(2,1)S(1)}, bf16[1,128,1280]{2,1,0:T(8,128)(2,1)S(1)}, u32[]{:S(2)}, u32[]{:S(2)}) collective-permute-start(bf16[1,128,1280]{2,1,0:T(8,128)(2,1)S(1)} %slice.41), channel_id=1, source_target_pairs={{0,1},{1,0},{2,3},{3,2},{4,5},{5,4},{6,7},{7,6},{8,9},{9,8},{10,11... | collective-permute-start | bytes 983048 | tf_op jit(solution)/shard_map/ppermute | solution.py:34
  85.5 3.6 %collective-permute-start.9 = (bf16[1,128,1280]{2,1,0:T(8,128)(2,1)}, bf16[1,128,1280]{2,1,0:T(8,128)(2,1)S(1)}, u32[]{:S(2)}, u32[]{:S(2)}) collective-permute-start(bf16[1,128,1280]{2,1,0:T(8,128)(2,1)} %collective-permute-done.5), channel_id=1, source_target_pairs={{0,1},{1,0},{2,3},{3,2},{4,5},{5,4},{6,7},{7,6},{8,9},{9,8},{10,11... | collective-permute-start | bytes 983048 | tf_op jit(solution)/shard_map/ppermute | solution.py:34
  85.6 3.5 %collective-permute-start.10 = (bf16[1,128,1280]{2,1,0:T(8,128)(2,1)S(1)}, bf16[1,128,1280]{2,1,0:T(8,128)(2,1)S(1)}, u32[]{:S(2)}, u32[]{:S(2)}) collective-permute-start(bf16[1,128,1280]{2,1,0:T(8,128)(2,1)S(1)} %slice.42), channel_id=1, source_target_pairs={{0,1},{1,0},{2,3},{3,2},{4,5},{5,4},{6,7},{7,6},{8,9},{9,8},{10,11... | collective-permute-start | bytes 983048 | tf_op jit(solution)/shard_map/ppermute | solution.py:34
  144.5 10.2 %all-to-all-start.3 = ((bf16[8,8,1280]{2,1,0:T(8,128)(2,1)}), bf16[8,8,1280]{2,1,0:T(8,128)(2,1)S(1)}, u32[]{:S(2)}, u32[]{:S(2)}) async-start(bf16[8,8,1280]{2,1,0:T(8,128)(2,1)} %bitcast.5), calls=%async_computation.3 | async-start | bytes 327680 | tf_op jit(solution)/shard_map/all_to_all | solution.py:418
  149.1 64.5 %all-gather.3.cloned.1.call-start = ((), (), s32[]{:S(2)}) async-start(), calls=%async_computation.7 | async-start | bytes 4325376 | tf_op jit(solution)/shard_map/all_gather | solution.py:434
  156.7 15.7 %copy-start.7 = (s32[64]{0:T(128)S(1)}, s32[64]{0:T(128)}, u32[]{:S(2)}) copy-start(s32[64]{0:T(128)} %reshape_squeeze.9.ids_ref) | copy-start | bytes 772
  173.0 13.4 %all-to-all-start.4 = ((s32[4,1,64]{2,1,0:T(1,128)}), s32[4,1,64]{2,1,0:T(1,128)S(1)}, u32[]{:S(2)}, u32[]{:S(2)}) async-start(s32[4,1,64]{2,1,0:T(1,128)} %broadcast_in_dim.44), calls=%async_computation.4 | async-start | bytes 4096 | tf_op jit(solution)/shard_map/all_to_all | solution.py:437
  183.7 42.8 %collective-permute-start.11 = (bf16[128,2048]{1,0:T(8,128)(2,1)}, bf16[128,2048]{1,0:T(8,128)(2,1)S(1)}, u32[]{:S(2)}, u32[]{:S(2)}) collective-permute-start(bf16[128,2048]{1,0:T(8,128)(2,1)} %get-tuple-element.57), channel_id=1, source_target_pairs={{0,32},{32,64},{64,96},{96,0},{1,33},{33,65},{65,97},{97,1},{2,34}... | collective-permute-start | bytes 1572872 | tf_op jit(solution)/shard_map/ppermute | solution.py:30
  183.7 42.8 %collective-permute-start.12 = (bf16[128,2048]{1,0:T(8,128)(2,1)S(1)}, bf16[128,2048]{1,0:T(8,128)(2,1)S(1)}, u32[]{:S(2)}, u32[]{:S(2)}) collective-permute-start(bf16[128,2048]{1,0:T(8,128)(2,1)S(1)} %get-tuple-element.56), channel_id=1, source_target_pairs={{0,64},{32,96},{64,0},{96,32},{1,65},{33,97},{65,1},{97,33},{2,66}... | collective-permute-start | bytes 1572872 | tf_op jit(solution)/shard_map/ppermute | solution.py:30
  184.5 42.1 %collective-permute-start.13 = (bf16[128,2048]{1,0:T(8,128)(2,1)S(1)}, bf16[128,2048]{1,0:T(8,128)(2,1)S(1)}, u32[]{:S(2)}, u32[]{:S(2)}) collective-permute-start(bf16[128,2048]{1,0:T(8,128)(2,1)S(1)} %get-tuple-element.55), channel_id=1, source_target_pairs={{0,96},{32,0},{64,32},{96,64},{1,97},{33,1},{65,33},{97,65},{2,98}... | collective-permute-start | bytes 1572872 | tf_op jit(solution)/shard_map/ppermute | solution.py:30
  220.6 14.3 %all-to-all-start.5 = ((bf16[32,8,512]{2,1,0:T(8,128)(2,1)}), bf16[32,8,512]{2,1,0:T(8,128)(2,1)S(1)}, u32[]{:S(2)}, u32[]{:S(2)}) async-start(bf16[32,8,512]{2,1,0:T(8,128)(2,1)} %output_product.1), calls=%async_computation.5 | async-start | bytes 524288 | tf_op jit(solution)/shard_map/all_to_all | solution.py:441
  238.8 11.5 %all-to-all-start.6 = ((bf16[32,8,256]{2,1,0:T(8,128)(2,1)}), bf16[32,8,256]{2,1,0:T(8,128)(2,1)S(1)}, u32[]{:S(2)}, u32[]{:S(2)}) async-start(bf16[32,8,256]{2,1,0:T(8,128)(2,1)} %panel_order.1), calls=%async_computation.6 | async-start | bytes 262144 | tf_op jit(solution)/shard_map/all_to_all | solution.py:444
  (18 other events, 83.7 us)
Sparse Core Ops, SparseCore 0:
  29.9 123.4 all-gather.4
  169.4 44.1 all-gather.2

commit v2 on v1

--- a/solution.py
+++ b/solution.py
@@ -75,8 +75,8 @@
     )(place, panels, panels, panels)
 
 
-def project_kernel(core_ref, mine_ref, other_ref, *refs):
-    pieces, (out_ref, w_ref) = refs[:8], refs[8:]
+def project_kernel(core_ref, *refs):
+    rows, pieces, (out_ref, w_ref) = refs[:8], refs[8:16], refs[16:]
     core = core_ref[0]
 
     @pl.when(pl.program_id(0) == 0)
@@ -86,7 +86,8 @@
             at = pl.multiple_of((i // 2) * 256 + slot * 128, 128)
             w_ref[pl.ds(at, 128), :] = piece[0]
 
-    mine, other = mine_ref[...], other_ref[...]
+    mine = jnp.concatenate([r[...] for r in rows[:4]], axis=2)
+    other = jnp.concatenate([r[...] for r in rows[4:]], axis=2)
     low = core == 0
     x = jnp.concatenate([jnp.where(low, mine, other), jnp.where(low, other, mine)], axis=1)
     x = x.reshape(256, 1024)
@@ -96,15 +97,14 @@
 
 
 def project(core, mine, other, *pieces):
-    rows = pl.BlockSpec((4, 32, 1024), lambda i, c: (i, 0, 0))
+    rows = pl.BlockSpec((4, 32, 256), lambda i, c: (i, 0, 0))
     return pl.pallas_call(
         project_kernel,
         grid_spec=pltpu.PrefetchScalarGridSpec(
             num_scalar_prefetch=1,
             grid=(4,),
             in_specs=[
-                rows,
-                rows,
+                *[rows] * 8,
                 *[pl.BlockSpec((1, 2 * PR, GROUP), lambda i, c, at=at: (at, 0, 0)) for _, at in pieces],
             ],
             out_specs=pl.BlockSpec((4, 64, GROUP), lambda i, c: (i, 0, 0)),
@@ -114,7 +114,7 @@
         compiler_params=pltpu.CompilerParams(vmem_limit_bytes=VMEM),
         cost_estimate=pl.CostEstimate(flops=2_700_000_000, bytes_accessed=7_500_000, transcendentals=0),
         name="project",
-    )(core, mine, other, *[v for v, _ in pieces])
+    )(core, *mine, *other, *[v for v, _ in pieces])
 
 
 def output_kernel(x_ref, *refs):
@@ -150,17 +150,9 @@
     )(x, *[w] * 8)
 
 
-def pick_kernel(ids_ref, at_ref, first_ref, second_ref, gain_ref, out_ref, x_ref, scale_ref):
+def pick_kernel(ids_ref, core_ref, first_ref, second_ref, scale_ref, gain_ref, out_ref):
     e = pl.program_id(0)
-
-    @pl.when(e == 0)
-    def _():
-        x = jnp.concatenate([first_ref[...].astype(F32), second_ref[...].astype(F32)], axis=0)
-        x_ref[...] = x
-        mean = jnp.mean(x * x, axis=-1, keepdims=True)
-        scale_ref[...] = jnp.broadcast_to(lax.rsqrt(mean + 1e-06), (32, 128))
-
-    lane = lax.broadcasted_iota(jnp.int32, (32, 128), 1)
+    lane = lax.broadcasted_iota(jnp.int32, (4, 32, 128), 2)
     scale = scale_ref[...]
     new = lax.broadcasted_iota(jnp.int32, (32, 32), 0)
     old = lax.broadcasted_iota(jnp.int32, (32, 32), 1)
@@ -168,43 +160,47 @@
     turn = (old == source).astype(BF)
 
     def column(slot):
-        p = ids_ref[e * 16 + slot]
+        p = ids_ref[e * 4 + slot]
         valid = p < PANELS
         p = jnp.where(valid, p, 0)
         at = pl.multiple_of((p // 2) * 128, 128)
-        v = x_ref[:, pl.ds(at, 128)] * scale * gain_ref[:, pl.ds(at, 128)]
+        v = jnp.concatenate(
+            [r[:, 0, :, pl.ds(at, 128)].astype(F32) for r in (first_ref, second_ref)], axis=1
+        )
+        v = v * scale * gain_ref[:, pl.ds(at, 128)].reshape(1, 1, 128)
         return jnp.where(valid, v, 0.0), p % 2
 
-    for pair in range(8):
+    for pair in range(2):
         a, odd_a = column(2 * pair)
         b, odd_b = column(2 * pair + 1)
-        a = jnp.where(odd_a == 1, pltpu.roll(a, 64, 1), a)
-        b = jnp.where(odd_b == 0, pltpu.roll(b, 64, 1), b)
+        a = jnp.where(odd_a == 1, pltpu.roll(a, 64, 2), a)
+        b = jnp.where(odd_b == 0, pltpu.roll(b, 64, 2), b)
         both = jnp.where(lane < 64, a, b).astype(BF)
-        both = jnp.dot(turn, both, preferred_element_type=F32).astype(BF)
-        for z in range(4):
-            at = (pair // 2 - z) % 4 * 256 + pair % 2 * 128
-            out_ref[0, z, :, at : at + 128] = both
-
-
-def pick_columns(ids, at, first, second, gain):
+        for x in range(4):
+            turned = jnp.dot(turn, both[x], preferred_element_type=F32).astype(BF)
+            out_ref[0, x, :, pair * 128 : (pair + 1) * 128] = turned
+
+
+def pick_columns(ids, core, first, second, scale, gain):
+    half = pl.BlockSpec((4, 1, 16, D), lambda e, ids, c: (0, c[0], 0, 0))
     return pl.pallas_call(
         pick_kernel,
         grid_spec=pltpu.PrefetchScalarGridSpec(
             num_scalar_prefetch=2,
             grid=(4,),
             in_specs=[
-                pl.BlockSpec((16, D), lambda e, ids, at: (at[0], 0)),
-                pl.BlockSpec((16, D), lambda e, ids, at: (at[0], 0)),
-                pl.BlockSpec((1, D), lambda e, ids, at: (0, 0)),
-            ],
-            out_specs=pl.BlockSpec((1, 4, 32, 1024), lambda e, ids, at: (e, 0, 0, 0)),
-            scratch_shapes=[pltpu.VMEM((32, D), F32), pltpu.VMEM((32, 128), F32)],
-        ),
-        out_shape=jax.ShapeDtypeStruct((4, 4, 32, 1024), BF),
-        cost_estimate=pl.CostEstimate(flops=20_000_000, bytes_accessed=2_000_000, transcendentals=0),
+                half,
+                half,
+                pl.BlockSpec((4, 32, 1), lambda e, ids, c: (0, 0, 0)),
+                pl.BlockSpec((1, D), lambda e, ids, c: (0, 0)),
+            ],
+            out_specs=pl.BlockSpec((1, 4, 32, 256), lambda e, ids, c: (e, 0, 0, 0)),
+        ),
+        out_shape=jax.ShapeDtypeStruct((4, 4, 32, 256), BF),
+        compiler_params=pltpu.CompilerParams(vmem_limit_bytes=VMEM),
+        cost_estimate=pl.CostEstimate(flops=20_000_000, bytes_accessed=3_000_000, transcendentals=0),
         name="pick_columns",
-    )(ids, at, first, second, gain)
+    )(ids, core, first, second, scale, gain)
 
 
 def attend_kernel(table_ref, length_ref, q_ref, k_ref, v_ref, *refs):
@@ -375,35 +371,41 @@
     plane = ("x", "z", "c")
 
     right, far_a, far_b, left, own_a, own_b = split_heads(jnp.stack([z, c]), panels)
-    own_b = swap(own_b)
-
-    near = lax.all_to_all(
-        jnp.broadcast_to(panel_ids, (32, 8, 64, 2)).reshape(32, 8, 128), ("y", "z", "c"), 0, 0, tiled=True
-    )[:, 0, :2].reshape(64)
-    near, right, left, far_a, far_b, w_o = lax.optimization_barrier(
-        (near, right, left, far_a, far_b, panels[:, :, QKV:])
+    panel_ids, right, left, far_a, far_b, w_o = lax.optimization_barrier(
+        (panel_ids, right, left, far_a, far_b, panels[:, :, QKV:])
     )
     w_o = lax.all_gather(w_o, "y", axis=0, tiled=True)
     far_a = shift(far_a, "z", 1)
     far_b = shift(far_b, "z", -1)
     from_left = shift(right, "z", 1)
     from_right = shift(left, "z", -1)
-
-    block = (z * 2 + c).reshape(1)
-    picked = pick_columns(near, block, first, second, gain.reshape(1, D)).reshape(16, 32, 1024)
+    own_b = swap(own_b)
+
+    near = lax.all_to_all(jnp.broadcast_to(panel_ids[None], (8, 2)), ("y", "c"), 0, 0, tiled=True)
+    near = near.reshape(16)
+
+    values = jnp.stack([first.reshape(4, 2, 16, D), second.reshape(4, 2, 16, D)]).astype(F32)
+    scale = lax.rsqrt(jnp.mean(values * values, axis=-1) + 1e-06)
+    scale = lax.dynamic_index_in_dim(scale, c, 2, keepdims=False)
+    scale = scale.transpose(1, 0, 2).reshape(4, 32, 1)
+    picked = pick_columns(
+        near, c.reshape(1), first.reshape(4, 2, 16, D), second.reshape(4, 2, 16, D), scale, gain.reshape(1, D)
+    )
     picked, far_a, far_b = lax.optimization_barrier((picked, far_a, far_b))
     far_a = shift(far_a, "z", 1)
     far_b = shift(far_b, "z", -1)
-    rows = lax.all_to_all(picked, ("y", "z"), 0, 0, tiled=True)
-    rows, from_left, from_right, far_a, far_b = lax.optimization_barrier(
-        (rows, from_left, from_right, far_a, far_b)
-    )
+    rows = lax.all_to_all(picked, "y", 0, 0, tiled=True).reshape(16, 32, 256)
+    rows_left = shift(rows, "z", 1)
+    rows_right = shift(rows, "z", -1)
+    rows_far = jnp.concatenate([shift(rows_left[:8], "z", 1), shift(rows_right[8:], "z", -1)], axis=0)
+    mine = (rows, rows_right, rows_far, rows_left)
+    other = tuple(swap(v) for v in mine)
     left_b = swap(from_left[1:])
     right_b = swap(from_right[1:])
     partial = project(
         c.reshape(1),
-        rows,
-        swap(rows),
+        mine,
+        other,
         (own_a, 0),
         (own_b, 0),
         (from_right, 0),
@@ -414,6 +416,7 @@
         (left_b, 0),
     )
     parts = lax.all_to_all(partial, ("y", "x"), 0, 0, tiled=True)
+    parts, w_o = lax.optimization_barrier((parts, w_o))
     summed = jnp.sum(parts.astype(F32), axis=0).astype(BF)
     projected = lax.all_to_all(summed.reshape(8, 8, GROUP), ("z", "c"), 0, 0, tiled=True)
     projected = projected.reshape(KVH, 2, 4, GROUP)
@@ -434,13 +437,13 @@
     mixed = lax.all_gather(mixed, plane, axis=0, tiled=True)
     out = output_product(mixed, w_o)
 
-    ids = lax.all_to_all(jnp.broadcast_to(near[None], (4, 64)), "x", 0, 0, tiled=True)
+    ids = lax.all_to_all(jnp.broadcast_to(near[None], (16, 16)), ("x", "z"), 0, 0, tiled=True)
     match = ids.reshape(1, 256) == jnp.arange(PANELS, dtype=jnp.int32)[:, None]
     slot = jnp.sum(jnp.where(match, jnp.arange(256, dtype=jnp.int32)[None, :], 0), axis=1)
-    source = slot // 64 * 8 + slot // 2 % 8
+    source = slot // 16 * 2 + slot // 2 % 2
     arrived = lax.all_to_all(out, plane, 0, 0, tiled=True)
     arrived, *got = lax.optimization_barrier((arrived, *got))
-    ordered = panel_order(source, slot // 16 % 4, slot % 2, arrived)
+    ordered = panel_order(source, slot // 4 % 4, slot % 2, arrived)
     final = lax.all_to_all(ordered, plane, 0, 0, tiled=True).reshape(32, 2, 4, 256)
 
     hosted = jnp.zeros((4, BLK, 2 * KV), BF)

time: 260 us -> 254 us (0.977)
  waiting for transfers between devices: 81.4 us -> 56.7 us
  blocking collectives: 45.7 us -> 56.8 us
  starting transfers between devices: 46.8 us -> 55.8 us
  other arithmetic: 5.51 us -> 8.46 us
    ppermute x9 -> x13, waiting for transfers between devices: 32.6 us -> 4.31 us  [shift(): return lax.ppermute(v, axis, [(i, (i + k) % 4) for i in range(4)])]
    all_to_all x0 -> x1, blocking collectives: none -> 13.3 us  [per_device(): rows = lax.all_to_all(picked, 'y', 0, 0, tiled=True).reshape(16, 32, 256)]
    ppermute x5 -> x8, starting transfers between devices: 3.16 us -> 13.9 us  [swap(): return lax.ppermute(v, 'c', [(0, 1), (1, 0)])]
    all_to_all x3 -> x2, starting transfers between devices: 19.2 us -> 11.5 us  [the longest x1 5.97 us: per_device(): lax.all_to_all(jnp.broadcast_to(panel_ids[None], (8, 2)), ('y', 'c'), 0,...]
    ppermute x9 -> x13, starting transfers between devices: 10.8 us -> 16.2 us  [shift(): return lax.ppermute(v, axis, [(i, (i + k) % 4) for i in range(4)])]
    all_gather x1, waiting for transfers between devices: 0.01 us -> 3.79 us  [per_device(): w_o = lax.all_gather(w_o, 'y', axis=0, tiled=True)]
    unnamed x41 -> x52, local copies, waits for them, and re-layouts: 5.64 us -> 3.71 us
  transfers between devices with their start and end apart: 22 -> 28, of which waited for: 10 -> 12; matrix products, arithmetic and copies ran while one was open for 7% -> 6% of each run, Pallas kernels for 16% -> 9%
where the time goes in v2:
time: 254 us; the launch traced here: 253 us
  blocking collectives  56.8 us (22%)
  waiting for transfers between devices  56.7 us (22%)
  starting transfers between devices  55.8 us (22%)
  Pallas kernels  42.2 us (17%)
  local copies, waits for them, and re-layouts  18.9 us (7%)
  between operations  14.5 us (6%)
  other arithmetic  8.46 us (3%)
    all_to_all x1, blocking collectives, per_device(): parts = lax.all_to_all(partial, ('y', 'x'), 0, 0, tiled=True)  43.5 us
    all_gather x1, waiting for transfers between devices, per_device(): mixed = lax.all_gather(mixed, plane, axis=0, tiled=True)  26.9 us
    ppermute x13, starting transfers between devices, shift(): return lax.ppermute(v, axis, [(i, (i + k) % 4) for i in range(4)])  16.2 us
    ppermute x8, starting transfers between devices, swap(): return lax.ppermute(v, 'c', [(0, 1), (1, 0)])  13.9 us
    all_to_all x1, blocking collectives, per_device(): rows = lax.all_to_all(picked, 'y', 0, 0, tiled=True).reshape(16, 32, 256)  13.3 us
    pallas_call x1, Pallas kernels, attend(): pl.pallas_call(attend_kernel, grid_spec=pltpu.PrefetchScalarGridSpec(num_...  8.79 us
    all_to_all x1, waiting for transfers between devices, per_device(): arrived = lax.all_to_all(out, plane, 0, 0, tiled=True)  8.31 us
    pallas_call x1, Pallas kernels, split_heads(): pl.pallas_call(split_kernel, grid_spec=pltpu.PrefetchScalarGridSpec(num_s...  7.06 us
  transfers between devices with their start and end apart: 28, of which 12 were waited for; matrix products, arithmetic and copies ran while one was open for 6% of the time, Pallas kernels for 9%

profile of v2, /device:TPU:1, one launch (start us, length us, event | category | flops | bytes accessed | tf_op | source)
XLA Modules:
  0.0 253.3 jit_solution(4008583645472821995)
XLA Ops:
  7.2 3.1 %slice.42 = bf16[2,64,8192]{2,1,0:T(8,128)(2,1)} slice(bf16[2,64,18432]{2,1,0:T(8,128)(2,1)} %v_ref.1), slice={[0:2], [0:64], [10240:18432]} | slice | bytes 4194304 | tf_op jit(solution)/shard_map/slice | solution.py:375
  10.9 7.1 %split_heads.1 = (bf16[2,128,1280]{2,1,0:T(8,128)(2,1)}, bf16[1,128,1280]{2,1,0:T(8,128)(2,1)}, bf16[1,128,1280]{2,1,0:T(8,128)(2,1)}, bf16[2,128,1280]{2,1,0:T(...) custom-call(s32[2]{0:T(128)} %pad_add_fusion.place_ref, bf16[2,64,18432]{2,1,0:T(8,128)(2,1)} %v_ref.1, ...), custom_call_target="tpu_custom_call" | custom-call | bytes 5300000 | tf_op jit(solution)/shard_map/split_heads/pallas_call | solution.py:60
  19.2 6.0 %all-to-all-start = ((s32[8,1,2]{2,1,0:T(1,128)}), s32[8,1,2]{2,1,0:T(1,128)S(1)}, u32[]{:S(2)}, u32[]{:S(2)}) async-start(s32[8,1,2]{2,1,0:T(1,128)} %broadcast_in_dim.40), calls=%async_computation | async-start | bytes 8192 | tf_op jit(solution)/shard_map/all_to_all | solution.py:384
  35.4 4.7 %pick_columns.1 = bf16[4,4,32,256]{3,2,1,0:T(8,128)(2,1)} custom-call(s32[16]{0:T(128)} %reshape.92.ids_ref, s32[1]{0:T(128)} %bitcast.core_ref, bf16[4,2,16,8192]{3,2,1,0:T(8,128)(2,1)} %bitcast.63, bf16[4,2,16,8192]{3,2,1,0:T(8,128)(2,1)} %bitcast.66, f32[4,32,1]{2,1,0:T(8,128)} %reshape.108.scale_ref, f32[1,8192]{1,0:T(1,128)} %bitcast.76), custom_call_target="tpu_custom_call" | custom-call | flops 20000000 | bytes 3000000 | tf_op jit(solution)/shard_map/pick_columns/pallas_call | solution.py:186
  40.1 13.3 %all_to_all.37 = bf16[4,4,32,256]{3,2,1,0:T(8,128)(2,1)S(1)} all-to-all(bf16[4,4,32,256]{3,2,1,0:T(8,128)(2,1)} %pick_columns.1), channel_id=1, replica_groups=mesh['y'=4,'x'=4,'z'=4,'c'=2] {'y'}, dimensions={0} | all-to-all | bytes 524288 | tf_op jit(solution)/shard_map/all_to_all | solution.py:397
  56.1 2.8 %collective-permute-start.2 = (bf16[16,32,256]{2,1,0:T(8,128)(2,1)S(1)}, bf16[16,32,256]{2,1,0:T(8,128)(2,1)S(1)}, u32[]{:S(2)}, u32[]{:S(2)}) collective-permute-start(bf16[16,32,256]{2,1,0:T(8,128)(2,1)S(1)} %bitcast.71), channel_id=1, source_target_pairs={{0,6},{2,0},{4,2},{6,4},{1,7},{3,1},{5,3},{7,5},{8,14},{10,8},{12,... | collective-permute-start | bytes 786440 | tf_op jit(solution)/shard_map/ppermute | solution.py:30
  62.1 3.7 %collective-permute-start.12 = (bf16[1,128,1280]{2,1,0:T(8,128)(2,1)S(1)}, bf16[1,128,1280]{2,1,0:T(8,128)(2,1)S(1)}, u32[]{:S(2)}, u32[]{:S(2)}) collective-permute-start(bf16[1,128,1280]{2,1,0:T(8,128)(2,1)S(1)} %slice.58), channel_id=1, source_target_pairs={{0,1},{1,0},{2,3},{3,2},{4,5},{5,4},{6,7},{7,6},{8,9},{9,8},{10,11... | collective-permute-start | bytes 983048 | tf_op jit(solution)/shard_map/ppermute | solution.py:34
  70.7 3.1 %collective-permute-start.17 = (bf16[1,128,1280]{2,1,0:T(8,128)(2,1)S(1)}, bf16[1,128,1280]{2,1,0:T(8,128)(2,1)S(1)}, u32[]{:S(2)}, u32[]{:S(2)}) collective-permute-start(bf16[1,128,1280]{2,1,0:T(8,128)(2,1)S(1)} %slice.59), channel_id=1, source_target_pairs={{0,1},{1,0},{2,3},{3,2},{4,5},{5,4},{6,7},{7,6},{8,9},{9,8},{10,11... | collective-permute-start | bytes 983048 | tf_op jit(solution)/shard_map/ppermute | solution.py:34
  73.9 3.7 %collective-permute-start.15 = (bf16[1,128,1280]{2,1,0:T(8,128)(2,1)S(1)}, bf16[1,128,1280]{2,1,0:T(8,128)(2,1)S(1)}, u32[]{:S(2)}, u32[]{:S(2)}) collective-permute-start(bf16[1,128,1280]{2,1,0:T(8,128)(2,1)S(1)} %collective-permute-done.14), channel_id=1, source_target_pairs={{0,1},{1,0},{2,3},{3,2},{4,5},{5,4},{6,7},{7,6},{8,9},{9,8},{10,11... | collective-permute-start | bytes 983048 | tf_op jit(solution)/shard_map/ppermute | solution.py:34
  81.0 7.0 %project.1 = bf16[16,64,1280]{2,1,0:T(8,128)(2,1)} custom-call(s32[1]{0:T(128)} %bitcast.core_ref, bf16[16,32,256]{2,1,0:T(8,128)(2,1)} %bitcast.73, bf16[16,32,256]{2,1,0:T(8,128)(2,1)} %copy-done.9, bf16[16,32,256]{2,1,0:T(8,128)(2,1)} %copy-done.10, bf16[16,32,256]{2,1,0:T(8,128)(2,1)} %copy-done.8, bf16[16,32,256]{2,1,0:T(8,128)(2,1)} %copy-done.21, ...), custom_call_target="tpu_custom_call" | custom-call | flops 2700000000 | bytes 7500000 | tf_op jit(solution)/shard_map/project/pallas_call | solution.py:101
  88.1 43.5 %all_to_all.38 = bf16[16,64,1280]{2,1,0:T(8,128)(2,1)S(1)} all-to-all(bf16[16,64,1280]{2,1,0:T(8,128)(2,1)} %project.1), channel_id=1, replica_groups=mesh['y'=4,'x'=4,'z'=4,'c'=2] {'y','x'}, dimensions={0} | all-to-all | bytes 5242880 | tf_op jit(solution)/shard_map/all_to_all | solution.py:418
  131.6 3.8 %all-gather.3.cloned.1.call-done.refs_0_.refs_1_.refs_2_.refs_3_.refs_4_.refs_5_.refs_6_.refs_7_ = bf16[8,64,8192]{2,1,0:T(8,128)(2,1)} async-done(((bf16[2,64,8192]{2,1,0:T(8,128)(2,1)}), bf16[8,64,8192]{2,1,0:T(8,128)(2,1)}) %all-gather.3.cloned.1.call-update) | async-done | bytes 8388624 | tf_op jit(solution)/shard_map/all_gather | solution.py:377
  136.4 5.1 %all-to-all-start.3 = ((bf16[8,8,1280]{2,1,0:T(8,128)(2,1)}), bf16[8,8,1280]{2,1,0:T(8,128)(2,1)S(1)}, u32[]{:S(2)}, u32[]{:S(2)}) async-start(bf16[8,8,1280]{2,1,0:T(8,128)(2,1)} %bitcast.10), calls=%async_computation.3 | async-start | bytes 327680 | tf_op jit(solution)/shard_map/all_to_all | solution.py:421
  142.2 5.0 %all-to-all-done.3 = bf16[8,8,1280]{2,1,0:T(8,128)(2,1)S(1)} async-done(((bf16[8,8,1280]{2,1,0:T(8,128)(2,1)}), bf16[8,8,1280]{2,1,0:T(8,128)(2,1)S(1)}, u32[]{:S(2)}, u32[]{:S(2)}) %all-to-all-start.3) | async-done | bytes 163872 | tf_op jit(solution)/shard_map/all_to_all | solution.py:421
  149.2 8.8 %attend.1 = bf16[4,8,16,128]{3,2,1,0:T(8,128)(2,1)} custom-call(s32[24]{0:T(128)} %reshape.90.table_ref, s32[4]{0:T(128)} %length_ref.3, bf16[4,8,16,128]{3,2,1,0:T(8,128)(2,1)} %bitcast.69, bf16[4,2,1024]{2,1,0:T(2,128)(2,1)} %copy.47.k_ref, bf16[4,2,1024]{2,1,0:T(2,128)(2,1)} %copy.48.v_ref, bf16[24,128,2048]{2,1,0:T(8,128)(2,1)} %bitcast.56, ...), custom_call_target="tpu_custom_call" | custom-call | flops 200000000 | bytes 13000000 | tf_op jit(solution)/shard_map/attend/pallas_call | solution.py:272
  163.4 5.6 %all-to-all-start.4 = ((s32[16,1,16]{2,1,0:T(1,128)}), s32[16,1,16]{2,1,0:T(1,128)S(1)}, u32[]{:S(2)}, u32[]{:S(2)}) async-start(s32[16,1,16]{2,1,0:T(1,128)} %broadcast_in_dim.41), calls=%async_computation.4 | async-start | bytes 16384 | tf_op jit(solution)/shard_map/all_to_all | solution.py:440
  169.6 4.4 %moved_blocks.1 = bf16[3,128,2048]{2,1,0:T(8,128)(2,1)} custom-call(s32[3]{0:T(128)} %pad_add_fusion.1.want_ref, s32[24]{0:T(128)} %reshape.90.table_ref, s32[4]{0:T(128)} %length_ref.3, bf16[8,2048]{1,0:T(8,128)(2,1)} %bitcast.74, bf16[24,128,2048]{2,1,0:T(8,128)(2,1)} %bitcast.62), custom_call_target="tpu_custom_call" | custom-call | flops 1000000 | bytes 3200000 | tf_op jit(solution)/shard_map/moved_blocks/pallas_call | solution.py:316
  181.6 26.9 %all-gather.5.cloned.1.call-done.x_ref = bf16[256,8192]{1,0:T(8,128)(2,1)} async-done(((bf16[8,8192]{1,0:T(8,128)(2,1)}), bf16[256,8192]{1,0:T(8,128)(2,1)}) %all-gather.5.cloned.1.call-update) | async-done | bytes 4194320 | tf_op jit(solution)/shard_map/all_gather | solution.py:437
  208.4 7.0 %output_product.1 = bf16[32,8,512]{2,1,0:T(8,128)(2,1)} custom-call(bf16[256,8192]{1,0:T(8,128)(2,1)} %all-gather.5.cloned.1.call-done.x_ref, bf16[8,64,8192]{2,1,0:T(8,128)(2,1)} %all-gather.3.cloned.1.call-done.refs_0_.refs_1_.refs_2_.refs_3_.refs_4_.refs_5_.refs_6_.refs_7_, ...), custom_call_target="tpu_custom_call" | custom-call | flops 2150000128 | bytes 12800000 | tf_op jit(solution)/shard_map/output_product/pallas_call | solution.py:137
  215.5 5.3 %all-to-all-start.5 = ((bf16[32,8,512]{2,1,0:T(8,128)(2,1)}), bf16[32,8,512]{2,1,0:T(8,128)(2,1)S(1)}, u32[]{:S(2)}, u32[]{:S(2)}) async-start(bf16[32,8,512]{2,1,0:T(8,128)(2,1)} %output_product.1), calls=%async_computation.5 | async-start | bytes 524288 | tf_op jit(solution)/shard_map/all_to_all | solution.py:444
  221.4 8.3 %all-to-all-done.5.in_ref = bf16[32,8,512]{2,1,0:T(8,128)(2,1)S(1)} async-done(((bf16[32,8,512]{2,1,0:T(8,128)(2,1)}), bf16[32,8,512]{2,1,0:T(8,128)(2,1)S(1)}, u32[]{:S(2)}, u32[]{:S(2)}) %all-to-all-start.5) | async-done | bytes 262176 | tf_op jit(solution)/shard_map/all_to_all | solution.py:444
  230.5 3.1 %panel_order.1 = bf16[32,8,256]{2,1,0:T(8,128)(2,1)} custom-call(s32[128]{0:T(128)} %get-tuple-element.60.from_ref, s32[128]{0:T(128)} %get-tuple-element.61.at_ref, s32[128]{0:T(128)} %get-tuple-element.59.half_ref, bf16[32,8,512]{2,1,0:T(8,128)(2,1)} %copy-done.2), custom_call_target="tpu_custom_call" | custom-call | tf_op jit(solution)/shard_map/panel_order/pallas_call | solution.py:353
  233.6 3.7 %all-to-all-start.6 = ((bf16[32,8,256]{2,1,0:T(8,128)(2,1)}), bf16[32,8,256]{2,1,0:T(8,128)(2,1)S(1)}, u32[]{:S(2)}, u32[]{:S(2)}) async-start(bf16[32,8,256]{2,1,0:T(8,128)(2,1)} %panel_order.1), calls=%async_computation.6 | async-start | bytes 262144 | tf_op jit(solution)/shard_map/all_to_all | solution.py:447
  238.4 6.7 %all-to-all-done.6 = bf16[32,8,256]{2,1,0:T(8,128)(2,1)S(1)} async-done(((bf16[32,8,256]{2,1,0:T(8,128)(2,1)}), bf16[32,8,256]{2,1,0:T(8,128)(2,1)S(1)}, u32[]{:S(2)}, u32[]{:S(2)}) %all-to-all-start.6) | async-done | bytes 131104 | tf_op jit(solution)/shard_map/all_to_all | solution.py:447
  (140 shorter events, 47.2 us)
Async XLA Ops:
  7.2 128.2 %all-gather.3.cloned.1.call-start = ((), (), s32[]{:S(2)}) async-start(), calls=%async_computation.7 | async-start | bytes 10485760 | tf_op jit(solution)/shard_map/all_gather | solution.py:377
  19.2 14.4 %all-to-all-start = ((s32[8,1,2]{2,1,0:T(1,128)}), s32[8,1,2]{2,1,0:T(1,128)S(1)}, u32[]{:S(2)}, u32[]{:S(2)}) async-start(s32[8,1,2]{2,1,0:T(1,128)} %broadcast_in_dim.40), calls=%async_computation | async-start | bytes 8192 | tf_op jit(solution)/shard_map/all_to_all | solution.py:384
  25.2 14.9 %collective-permute-start = (bf16[1,128,1280]{2,1,0:T(8,128)(2,1)}, bf16[1,128,1280]{2,1,0:T(8,128)(2,1)}, u32[]{:S(2)}, u32[]{:S(2)}) collective-permute-start(bf16[1,128,1280]{2,1,0:T(8,128)(2,1)} %get-tuple-element.31), channel_id=1, source_target_pairs={{0,2},{2,4},{4,6},{6,0},{1,3},{3,5},{5,7},{7,1},{8,10},{10,12},{12... | collective-permute-start | bytes 983048 | tf_op jit(solution)/shard_map/ppermute | solution.py:30
  26.8 13.3 %collective-permute-start.1 = (bf16[1,128,1280]{2,1,0:T(8,128)(2,1)}, bf16[1,128,1280]{2,1,0:T(8,128)(2,1)}, u32[]{:S(2)}, u32[]{:S(2)}) collective-permute-start(bf16[1,128,1280]{2,1,0:T(8,128)(2,1)} %get-tuple-element.32), channel_id=1, source_target_pairs={{0,6},{2,0},{4,2},{6,4},{1,7},{3,1},{5,3},{7,5},{8,14},{10,8},{12,... | collective-permute-start | bytes 983048 | tf_op jit(solution)/shard_map/ppermute | solution.py:30
  29.0 33.0 %collective-permute-start.11 = (bf16[2,128,1280]{2,1,0:T(8,128)(2,1)}, bf16[2,128,1280]{2,1,0:T(8,128)(2,1)S(1)}, u32[]{:S(2)}, u32[]{:S(2)}) collective-permute-start(bf16[2,128,1280]{2,1,0:T(8,128)(2,1)} %get-tuple-element.36), channel_id=1, source_target_pairs={{0,6},{2,0},{4,2},{6,4},{1,7},{3,1},{5,3},{7,5},{8,14},{10,8},{12,... | collective-permute-start | bytes 1966088 | tf_op jit(solution)/shard_map/ppermute | solution.py:30
  30.4 31.7 %collective-permute-start.16 = (bf16[2,128,1280]{2,1,0:T(8,128)(2,1)}, bf16[2,128,1280]{2,1,0:T(8,128)(2,1)S(1)}, u32[]{:S(2)}, u32[]{:S(2)}) collective-permute-start(bf16[2,128,1280]{2,1,0:T(8,128)(2,1)} %get-tuple-element.39), channel_id=1, source_target_pairs={{0,2},{2,4},{4,6},{6,0},{1,3},{3,5},{5,7},{7,1},{8,10},{10,12},{12... | collective-permute-start | bytes 1966088 | tf_op jit(solution)/shard_map/ppermute | solution.py:30
  53.4 6.9 %collective-permute-start.3 = (bf16[16,32,256]{2,1,0:T(8,128)(2,1)S(1)}, bf16[16,32,256]{2,1,0:T(8,128)(2,1)S(1)}, u32[]{:S(2)}, u32[]{:S(2)}) collective-permute-start(bf16[16,32,256]{2,1,0:T(8,128)(2,1)S(1)} %bitcast.70), channel_id=1, source_target_pairs={{0,2},{2,4},{4,6},{6,0},{1,3},{3,5},{5,7},{7,1},{8,10},{10,12},{12... | collective-permute-start | bytes 786440 | tf_op jit(solution)/shard_map/ppermute | solution.py:30
  53.5 8.4 %collective-permute-start.10 = (bf16[1,128,1280]{2,1,0:T(8,128)(2,1)S(1)}, bf16[1,128,1280]{2,1,0:T(8,128)(2,1)S(1)}, u32[]{:S(2)}, u32[]{:S(2)}) collective-permute-start(bf16[1,128,1280]{2,1,0:T(8,128)(2,1)S(1)} %copy-done.18), channel_id=1, source_target_pairs={{0,1},{1,0},{2,3},{3,2},{4,5},{5,4},{6,7},{7,6},{8,9},{9,8},{10,11... | collective-permute-start | bytes 983048 | tf_op jit(solution)/shard_map/ppermute | solution.py:34
  56.1 9.7 %collective-permute-start.2 = (bf16[16,32,256]{2,1,0:T(8,128)(2,1)S(1)}, bf16[16,32,256]{2,1,0:T(8,128)(2,1)S(1)}, u32[]{:S(2)}, u32[]{:S(2)}) collective-permute-start(bf16[16,32,256]{2,1,0:T(8,128)(2,1)S(1)} %bitcast.71), channel_id=1, source_target_pairs={{0,6},{2,0},{4,2},{6,4},{1,7},{3,1},{5,3},{7,5},{8,14},{10,8},{12,... | collective-permute-start | bytes 786440 | tf_op jit(solution)/shard_map/ppermute | solution.py:30
  60.4 10.4 %collective-permute-start.14 = (bf16[1,128,1280]{2,1,0:T(8,128)(2,1)}, bf16[1,128,1280]{2,1,0:T(8,128)(2,1)S(1)}, u32[]{:S(2)}, u32[]{:S(2)}) collective-permute-start(bf16[1,128,1280]{2,1,0:T(8,128)(2,1)} %collective-permute-done.1), channel_id=1, source_target_pairs={{0,6},{2,0},{4,2},{6,4},{1,7},{3,1},{5,3},{7,5},{8,14},{10,8},{12,... | collective-permute-start | bytes 983048 | tf_op jit(solution)/shard_map/ppermute | solution.py:30
  61.9 5.5 %collective-permute-start.4 = (bf16[8,32,256]{2,1,0:T(8,128)(2,1)S(1)}, bf16[8,32,256]{2,1,0:T(8,128)(2,1)S(1)}, u32[]{:S(2)}, u32[]{:S(2)}) collective-permute-start(bf16[8,32,256]{2,1,0:T(8,128)(2,1)S(1)} %slice.56), channel_id=1, source_target_pairs={{0,2},{2,4},{4,6},{6,0},{1,3},{3,5},{5,7},{7,1},{8,10},{10,12},{12... | collective-permute-start | bytes 393224 | tf_op jit(solution)/shard_map/ppermute | solution.py:30
  62.0 15.6 %collective-permute-start.13 = (bf16[1,128,1280]{2,1,0:T(8,128)(2,1)}, bf16[1,128,1280]{2,1,0:T(8,128)(2,1)S(1)}, u32[]{:S(2)}, u32[]{:S(2)}) collective-permute-start(bf16[1,128,1280]{2,1,0:T(8,128)(2,1)} %collective-permute-done), channel_id=1, source_target_pairs={{0,2},{2,4},{4,6},{6,0},{1,3},{3,5},{5,7},{7,1},{8,10},{10,12},{12... | collective-permute-start | bytes 983048 | tf_op jit(solution)/shard_map/ppermute | solution.py:30
  62.1 16.1 %collective-permute-start.12 = (bf16[1,128,1280]{2,1,0:T(8,128)(2,1)S(1)}, bf16[1,128,1280]{2,1,0:T(8,128)(2,1)S(1)}, u32[]{:S(2)}, u32[]{:S(2)}) collective-permute-start(bf16[1,128,1280]{2,1,0:T(8,128)(2,1)S(1)} %slice.58), channel_id=1, source_target_pairs={{0,1},{1,0},{2,3},{3,2},{4,5},{5,4},{6,7},{7,6},{8,9},{9,8},{10,11... | collective-permute-start | bytes 983048 | tf_op jit(solution)/shard_map/ppermute | solution.py:34
  65.8 11.8 %collective-permute-start.6 = (bf16[16,32,256]{2,1,0:T(8,128)(2,1)S(1)}, bf16[16,32,256]{2,1,0:T(8,128)(2,1)S(1)}, u32[]{:S(2)}, u32[]{:S(2)}) collective-permute-start(bf16[16,32,256]{2,1,0:T(8,128)(2,1)S(1)} %bitcast.72), channel_id=1, source_target_pairs={{0,1},{1,0},{2,3},{3,2},{4,5},{5,4},{6,7},{7,6},{8,9},{9,8},{10,11... | collective-permute-start | bytes 786440 | tf_op jit(solution)/shard_map/ppermute | solution.py:34
  67.4 6.5 %collective-permute-start.5 = (bf16[8,32,256]{2,1,0:T(8,128)(2,1)S(1)}, bf16[8,32,256]{2,1,0:T(8,128)(2,1)S(1)}, u32[]{:S(2)}, u32[]{:S(2)}) collective-permute-start(bf16[8,32,256]{2,1,0:T(8,128)(2,1)S(1)} %slice.57), channel_id=1, source_target_pairs={{0,6},{2,0},{4,2},{6,4},{1,7},{3,1},{5,3},{7,5},{8,14},{10,8},{12,... | collective-permute-start | bytes 393224 | tf_op jit(solution)/shard_map/ppermute | solution.py:30
  70.7 8.1 %collective-permute-start.17 = (bf16[1,128,1280]{2,1,0:T(8,128)(2,1)S(1)}, bf16[1,128,1280]{2,1,0:T(8,128)(2,1)S(1)}, u32[]{:S(2)}, u32[]{:S(2)}) collective-permute-start(bf16[1,128,1280]{2,1,0:T(8,128)(2,1)S(1)} %slice.59), channel_id=1, source_target_pairs={{0,1},{1,0},{2,3},{3,2},{4,5},{5,4},{6,7},{7,6},{8,9},{9,8},{10,11... | collective-permute-start | bytes 983048 | tf_op jit(solution)/shard_map/ppermute | solution.py:34
  136.4 10.7 %all-to-all-start.3 = ((bf16[8,8,1280]{2,1,0:T(8,128)(2,1)}), bf16[8,8,1280]{2,1,0:T(8,128)(2,1)S(1)}, u32[]{:S(2)}, u32[]{:S(2)}) async-start(bf16[8,8,1280]{2,1,0:T(8,128)(2,1)} %bitcast.10), calls=%async_computation.3 | async-start | bytes 327680 | tf_op jit(solution)/shard_map/all_to_all | solution.py:421
  141.6 66.9 %all-gather.5.cloned.1.call-start = ((), (), s32[]{:S(2)}) async-start(), calls=%async_computation.8 | async-start | bytes 4325376 | tf_op jit(solution)/shard_map/all_gather | solution.py:437
  163.4 17.4 %all-to-all-start.4 = ((s32[16,1,16]{2,1,0:T(1,128)}), s32[16,1,16]{2,1,0:T(1,128)S(1)}, u32[]{:S(2)}, u32[]{:S(2)}) async-start(s32[16,1,16]{2,1,0:T(1,128)} %broadcast_in_dim.41), calls=%async_computation.4 | async-start | bytes 16384 | tf_op jit(solution)/shard_map/all_to_all | solution.py:440
  176.2 45.2 %collective-permute-start.18 = (bf16[128,2048]{1,0:T(8,128)(2,1)}, bf16[128,2048]{1,0:T(8,128)(2,1)S(1)}, u32[]{:S(2)}, u32[]{:S(2)}) collective-permute-start(bf16[128,2048]{1,0:T(8,128)(2,1)} %get-tuple-element.51), channel_id=1, source_target_pairs={{0,32},{32,64},{64,96},{96,0},{1,33},{33,65},{65,97},{97,1},{2,34}... | collective-permute-start | bytes 1572872 | tf_op jit(solution)/shard_map/ppermute | solution.py:30
  178.4 43.0 %collective-permute-start.19 = (bf16[128,2048]{1,0:T(8,128)(2,1)S(1)}, bf16[128,2048]{1,0:T(8,128)(2,1)S(1)}, u32[]{:S(2)}, u32[]{:S(2)}) collective-permute-start(bf16[128,2048]{1,0:T(8,128)(2,1)S(1)} %get-tuple-element.50), channel_id=1, source_target_pairs={{0,64},{32,96},{64,0},{96,32},{1,65},{33,97},{65,1},{97,33},{2,66}... | collective-permute-start | bytes 1572872 | tf_op jit(solution)/shard_map/ppermute | solution.py:30
  179.0 42.5 %collective-permute-start.20 = (bf16[128,2048]{1,0:T(8,128)(2,1)S(1)}, bf16[128,2048]{1,0:T(8,128)(2,1)S(1)}, u32[]{:S(2)}, u32[]{:S(2)}) collective-permute-start(bf16[128,2048]{1,0:T(8,128)(2,1)S(1)} %get-tuple-element.49), channel_id=1, source_target_pairs={{0,96},{32,0},{64,32},{96,64},{1,97},{33,1},{65,33},{97,65},{2,98}... | collective-permute-start | bytes 1572872 | tf_op jit(solution)/shard_map/ppermute | solution.py:30
  215.5 14.3 %all-to-all-start.5 = ((bf16[32,8,512]{2,1,0:T(8,128)(2,1)}), bf16[32,8,512]{2,1,0:T(8,128)(2,1)S(1)}, u32[]{:S(2)}, u32[]{:S(2)}) async-start(bf16[32,8,512]{2,1,0:T(8,128)(2,1)} %output_product.1), calls=%async_computation.5 | async-start | bytes 524288 | tf_op jit(solution)/shard_map/all_to_all | solution.py:444
  233.6 11.5 %all-to-all-start.6 = ((bf16[32,8,256]{2,1,0:T(8,128)(2,1)}), bf16[32,8,256]{2,1,0:T(8,128)(2,1)S(1)}, u32[]{:S(2)}, u32[]{:S(2)}) async-start(bf16[32,8,256]{2,1,0:T(8,128)(2,1)} %panel_order.1), calls=%async_computation.6 | async-start | bytes 262144 | tf_op jit(solution)/shard_map/all_to_all | solution.py:447
  (29 other events, 235.2 us)
Sparse Core Ops, SparseCore 0:
  18.1 117.2 all-gather.2
  159.7 48.6 all-gather.4

commit v3 on v2

--- a/solution.py
+++ b/solution.py
@@ -400,8 +400,7 @@
     rows_far = jnp.concatenate([shift(rows_left[:8], "z", 1), shift(rows_right[8:], "z", -1)], axis=0)
     mine = (rows, rows_right, rows_far, rows_left)
     other = tuple(swap(v) for v in mine)
-    left_b = swap(from_left[1:])
-    right_b = swap(from_right[1:])
+    near_b = swap(jnp.concatenate([from_left[1:], from_right[1:]], axis=0))
     partial = project(
         c.reshape(1),
         mine,
@@ -409,16 +408,16 @@
         (own_a, 0),
         (own_b, 0),
         (from_right, 0),
-        (right_b, 0),
+        (near_b, 1),
         (far_a, 0),
         (swap(far_b), 0),
         (from_left, 0),
-        (left_b, 0),
+        (near_b, 0),
     )
     parts = lax.all_to_all(partial, ("y", "x"), 0, 0, tiled=True)
-    parts, w_o = lax.optimization_barrier((parts, w_o))
     summed = jnp.sum(parts.astype(F32), axis=0).astype(BF)
     projected = lax.all_to_all(summed.reshape(8, 8, GROUP), ("z", "c"), 0, 0, tiled=True)
+    projected, w_o = lax.optimization_barrier((projected, w_o))
     projected = projected.reshape(KVH, 2, 4, GROUP)
     query = projected[..., :1024].reshape(KVH, 2, 4, 8, HD).transpose(2, 0, 1, 3, 4)
     query = query.reshape(4, KVH, 16, HD)

time: 254 us -> 253 us (level)
  blocking collectives: 56.8 us -> 41.3 us
  waiting for transfers between devices: 56.7 us -> 65.2 us
  starting transfers between devices: 55.8 us -> 60.9 us
    all_to_all x1 -> x0, blocking collectives: 13.3 us -> none  [per_device(): rows = lax.all_to_all(picked, 'y', 0, 0, tiled=True).reshape(16, 32, 256)]
    all_to_all x0 -> x1, waiting for transfers between devices: none -> 8.58 us  [per_device(): rows = lax.all_to_all(picked, 'y', 0, 0, tiled=True).reshape(16, 32, 256)]
    ppermute x13, waiting for transfers between devices: 4.31 us -> 10.1 us  [shift(): return lax.ppermute(v, axis, [(i, (i + k) % 4) for i in range(4)])]
    all_to_all x0 -> x1, starting transfers between devices: none -> 4.18 us  [per_device(): rows = lax.all_to_all(picked, 'y', 0, 0, tiled=True).reshape(16, 32, 256)]
    all_gather x1, waiting for transfers between devices: 3.79 us -> 0.01 us  [per_device(): w_o = lax.all_gather(w_o, 'y', axis=0, tiled=True)]
    ppermute x8 -> x7, starting transfers between devices: 13.9 us -> 14.9 us  [swap(): return lax.ppermute(v, 'c', [(0, 1), (1, 0)])]
  transfers between devices with their start and end apart: 28 -> 28, of which waited for: 12 -> 11; matrix products, arithmetic and copies ran while one was open for 6% -> 6% of each run, Pallas kernels for 9% -> 9%
where the time goes in v3:
time: 253 us; the launch traced here: 252 us
  waiting for transfers between devices  65.2 us (26%)
  starting transfers between devices  60.9 us (24%)
  Pallas kernels  42.2 us (17%)
  blocking collectives  41.3 us (16%)
  local copies, waits for them, and re-layouts  18.8 us (7%)
  between operations  14.5 us (6%)
  other arithmetic  8.76 us (3%)
    all_to_all x1, blocking collectives, per_device(): parts = lax.all_to_all(partial, ('y', 'x'), 0, 0, tiled=True)  41.3 us
    all_gather x1, waiting for transfers between devices, per_device(): mixed = lax.all_gather(mixed, plane, axis=0, tiled=True)  25.1 us
    ppermute x13, starting transfers between devices, shift(): return lax.ppermute(v, axis, [(i, (i + k) % 4) for i in range(4)])  17 us
    ppermute x7, starting transfers between devices, swap(): return lax.ppermute(v, 'c', [(0, 1), (1, 0)])  14.9 us
    ppermute x13, waiting for transfers between devices, shift(): return lax.ppermute(v, axis, [(i, (i + k) % 4) for i in range(4)])  10.1 us
    pallas_call x1, Pallas kernels, attend(): pl.pallas_call(attend_kernel, grid_spec=pltpu.PrefetchScalarGridSpec(num_...  9.14 us
    all_to_all x1, waiting for transfers between devices, per_device(): rows = lax.all_to_all(picked, 'y', 0, 0, tiled=True).reshape(16, 32, 256)  8.58 us
    all_to_all x1, waiting for transfers between devices, per_device(): arrived = lax.all_to_all(out, plane, 0, 0, tiled=True)  8.23 us
  transfers between devices with their start and end apart: 28, of which 11 were waited for; matrix products, arithmetic and copies ran while one was open for 6% of the time, Pallas kernels for 9%

profile of v3, /device:TPU:1, one launch (start us, length us, event | category | flops | bytes accessed | tf_op | source)
XLA Modules:
  0.0 251.7 jit_solution(13192891625065481677)
XLA Ops:
  10.9 7.0 %split_heads.1 = (bf16[2,128,1280]{2,1,0:T(8,128)(2,1)}, bf16[1,128,1280]{2,1,0:T(8,128)(2,1)}, bf16[1,128,1280]{2,1,0:T(8,128)(2,1)}, bf16[2,128,1280]{2,1,0:T(...) custom-call(s32[2]{0:T(128)} %pad_add_fusion.place_ref, bf16[2,64,18432]{2,1,0:T(8,128)(2,1)} %v_ref.1, ...), custom_call_target="tpu_custom_call" | custom-call | bytes 5300000 | tf_op jit(solution)/shard_map/split_heads/pallas_call | solution.py:60
  18.0 4.7 %collective-permute-start.11 = (bf16[2,128,1280]{2,1,0:T(8,128)(2,1)}, bf16[2,128,1280]{2,1,0:T(8,128)(2,1)S(1)}, u32[]{:S(2)}, u32[]{:S(2)}) collective-permute-start(bf16[2,128,1280]{2,1,0:T(8,128)(2,1)} %get-tuple-element.36), channel_id=1, source_target_pairs={{0,6},{2,0},{4,2},{6,4},{1,7},{3,1},{5,3},{7,5},{8,14},{10,8},{12,... | collective-permute-start | bytes 1966088 | tf_op jit(solution)/shard_map/ppermute | solution.py:30
  23.2 5.4 %all-to-all-start = ((s32[8,1,2]{2,1,0:T(1,128)}), s32[8,1,2]{2,1,0:T(1,128)S(1)}, u32[]{:S(2)}, u32[]{:S(2)}) async-start(s32[8,1,2]{2,1,0:T(1,128)} %broadcast_in_dim.40), calls=%async_computation | async-start | bytes 8192 | tf_op jit(solution)/shard_map/all_to_all | solution.py:384
  36.6 4.4 %pick_columns.1 = bf16[4,4,32,256]{3,2,1,0:T(8,128)(2,1)} custom-call(s32[16]{0:T(128)} %reshape.92.ids_ref, s32[1]{0:T(128)} %bitcast.core_ref, bf16[4,2,16,8192]{3,2,1,0:T(8,128)(2,1)} %bitcast.63, bf16[4,2,16,8192]{3,2,1,0:T(8,128)(2,1)} %bitcast.66, f32[4,32,1]{2,1,0:T(8,128)} %reshape.108.scale_ref, f32[1,8192]{1,0:T(1,128)} %bitcast.76), custom_call_target="tpu_custom_call" | custom-call | flops 20000000 | bytes 3000000 | tf_op jit(solution)/shard_map/pick_columns/pallas_call | solution.py:186
  41.0 5.5 %collective-permute-done = bf16[1,128,1280]{2,1,0:T(8,128)(2,1)} collective-permute-done((bf16[1,128,1280]{2,1,0:T(8,128)(2,1)}, bf16[1,128,1280]{2,1,0:T(8,128)(2,1)}, u32[]{:S(2)}, u32[]{:S(2)}) %collective-permute-start) | collective-permute-done | bytes 327712 | tf_op jit(solution)/shard_map/ppermute | solution.py:30
  46.5 4.2 %all-to-all-start.1 = ((bf16[4,4,32,256]{3,2,1,0:T(8,128)(2,1)}), bf16[4,4,32,256]{3,2,1,0:T(8,128)(2,1)S(1)}, u32[]{:S(2)}, u32[]{:S(2)}) async-start(bf16[4,4,32,256]{3,2,1,0:T(8,128)(2,1)} %pick_columns.1), calls=%async_computation.1 | async-start | bytes 524288 | tf_op jit(solution)/shard_map/all_to_all | solution.py:397
  51.0 8.6 %all-to-all-done.1 = bf16[4,4,32,256]{3,2,1,0:T(8,128)(2,1)S(1)} async-done(((bf16[4,4,32,256]{3,2,1,0:T(8,128)(2,1)}), bf16[4,4,32,256]{3,2,1,0:T(8,128)(2,1)S(1)}, u32[]{:S(2)}, u32[]{:S(2)}) %all-to-all-start.1) | async-done | bytes 262176 | tf_op jit(solution)/shard_map/all_to_all | solution.py:397
  61.2 3.9 %collective-permute-start.13 = (bf16[2,128,1280]{2,1,0:T(8,128)(2,1)S(1)}, bf16[2,128,1280]{2,1,0:T(8,128)(2,1)S(1)}, u32[]{:S(2)}, u32[]{:S(2)}) collective-permute-start(bf16[2,128,1280]{2,1,0:T(8,128)(2,1)S(1)} %pad_maximum_fusion), channel_id=1, source_target_pairs={{0,1},{1,0},{2,3},{3,2},{4,5},{5,4},{6,7},{7,6},{8,9},{9,8},{10,11... | collective-permute-start | bytes 1966088 | tf_op jit(solution)/shard_map/ppermute | solution.py:34
  66.9 5.2 %collective-permute-start.10 = (bf16[1,128,1280]{2,1,0:T(8,128)(2,1)S(1)}, bf16[1,128,1280]{2,1,0:T(8,128)(2,1)S(1)}, u32[]{:S(2)}, u32[]{:S(2)}) collective-permute-start(bf16[1,128,1280]{2,1,0:T(8,128)(2,1)S(1)} %copy-done.16), channel_id=1, source_target_pairs={{0,1},{1,0},{2,3},{3,2},{4,5},{5,4},{6,7},{7,6},{8,9},{9,8},{10,11... | collective-permute-start | bytes 983048 | tf_op jit(solution)/shard_map/ppermute | solution.py:34
  77.3 5.0 %collective-permute-start.16 = (bf16[1,128,1280]{2,1,0:T(8,128)(2,1)}, bf16[1,128,1280]{2,1,0:T(8,128)(2,1)S(1)}, u32[]{:S(2)}, u32[]{:S(2)}) collective-permute-start(bf16[1,128,1280]{2,1,0:T(8,128)(2,1)} %copy-done.17), channel_id=1, source_target_pairs={{0,1},{1,0},{2,3},{3,2},{4,5},{5,4},{6,7},{7,6},{8,9},{9,8},{10,11... | collective-permute-start | bytes 983048 | tf_op jit(solution)/shard_map/ppermute | solution.py:34
  86.6 7.0 %project.1 = bf16[16,64,1280]{2,1,0:T(8,128)(2,1)} custom-call(s32[1]{0:T(128)} %bitcast.core_ref, bf16[16,32,256]{2,1,0:T(8,128)(2,1)} %bitcast.73, bf16[16,32,256]{2,1,0:T(8,128)(2,1)} %copy-done.8, bf16[16,32,256]{2,1,0:T(8,128)(2,1)} %copy-done.10, bf16[16,32,256]{2,1,0:T(8,128)(2,1)} %copy-done.9, bf16[16,32,256]{2,1,0:T(8,128)(2,1)} %copy-done.21, ...), custom_call_target="tpu_custom_call" | custom-call | flops 2700000000 | bytes 7500000 | tf_op jit(solution)/shard_map/project/pallas_call | solution.py:101
  93.6 41.3 %all_to_all.37 = bf16[16,64,1280]{2,1,0:T(8,128)(2,1)S(1)} all-to-all(bf16[16,64,1280]{2,1,0:T(8,128)(2,1)} %project.1), channel_id=1, replica_groups=mesh['y'=4,'x'=4,'z'=4,'c'=2] {'y','x'}, dimensions={0} | all-to-all | bytes 5242880 | tf_op jit(solution)/shard_map/all_to_all | solution.py:417
  135.9 5.3 %all-to-all-start.3 = ((bf16[8,8,1280]{2,1,0:T(8,128)(2,1)}), bf16[8,8,1280]{2,1,0:T(8,128)(2,1)S(1)}, u32[]{:S(2)}, u32[]{:S(2)}) async-start(bf16[8,8,1280]{2,1,0:T(8,128)(2,1)} %bitcast.10), calls=%async_computation.3 | async-start | bytes 327680 | tf_op jit(solution)/shard_map/all_to_all | solution.py:419
  141.9 5.0 %all-to-all-done.3 = bf16[8,8,1280]{2,1,0:T(8,128)(2,1)S(1)} async-done(((bf16[8,8,1280]{2,1,0:T(8,128)(2,1)}), bf16[8,8,1280]{2,1,0:T(8,128)(2,1)S(1)}, u32[]{:S(2)}, u32[]{:S(2)}) %all-to-all-start.3) | async-done | bytes 163872 | tf_op jit(solution)/shard_map/all_to_all | solution.py:419
  148.9 9.1 %attend.1 = bf16[4,8,16,128]{3,2,1,0:T(8,128)(2,1)} custom-call(s32[24]{0:T(128)} %reshape.90.table_ref, s32[4]{0:T(128)} %length_ref.3, bf16[4,8,16,128]{3,2,1,0:T(8,128)(2,1)} %bitcast.69, bf16[4,2,1024]{2,1,0:T(2,128)(2,1)} %copy.47.k_ref, bf16[4,2,1024]{2,1,0:T(2,128)(2,1)} %copy.48.v_ref, bf16[24,128,2048]{2,1,0:T(8,128)(2,1)} %bitcast.56, ...), custom_call_target="tpu_custom_call" | custom-call | flops 200000000 | bytes 13000000 | tf_op jit(solution)/shard_map/attend/pallas_call | solution.py:272
  163.5 5.1 %all-to-all-start.4 = ((s32[16,1,16]{2,1,0:T(1,128)}), s32[16,1,16]{2,1,0:T(1,128)S(1)}, u32[]{:S(2)}, u32[]{:S(2)}) async-start(s32[16,1,16]{2,1,0:T(1,128)} %broadcast_in_dim.41), calls=%async_computation.4 | async-start | bytes 16384 | tf_op jit(solution)/shard_map/all_to_all | solution.py:439
  169.2 4.4 %moved_blocks.1 = bf16[3,128,2048]{2,1,0:T(8,128)(2,1)} custom-call(s32[3]{0:T(128)} %pad_add_fusion.1.want_ref, s32[24]{0:T(128)} %reshape.90.table_ref, s32[4]{0:T(128)} %length_ref.3, bf16[8,2048]{1,0:T(8,128)(2,1)} %bitcast.74, bf16[24,128,2048]{2,1,0:T(8,128)(2,1)} %bitcast.62), custom_call_target="tpu_custom_call" | custom-call | flops 1000000 | bytes 3200000 | tf_op jit(solution)/shard_map/moved_blocks/pallas_call | solution.py:316
  181.7 25.1 %all-gather.5.cloned.1.call-done.x_ref = bf16[256,8192]{1,0:T(8,128)(2,1)} async-done(((bf16[8,8192]{1,0:T(8,128)(2,1)}), bf16[256,8192]{1,0:T(8,128)(2,1)}) %all-gather.5.cloned.1.call-update) | async-done | bytes 4194320 | tf_op jit(solution)/shard_map/all_gather | solution.py:436
  206.8 7.1 %output_product.1 = bf16[32,8,512]{2,1,0:T(8,128)(2,1)} custom-call(bf16[256,8192]{1,0:T(8,128)(2,1)} %all-gather.5.cloned.1.call-done.x_ref, bf16[8,64,8192]{2,1,0:T(8,128)(2,1)} %all-gather.3.cloned.1.call-done.refs_0_.refs_1_.refs_2_.refs_3_.refs_4_.refs_5_.refs_6_.refs_7_, ...), custom_call_target="tpu_custom_call" | custom-call | flops 2150000128 | bytes 12800000 | tf_op jit(solution)/shard_map/output_product/pallas_call | solution.py:137
  213.8 5.3 %all-to-all-start.5 = ((bf16[32,8,512]{2,1,0:T(8,128)(2,1)}), bf16[32,8,512]{2,1,0:T(8,128)(2,1)S(1)}, u32[]{:S(2)}, u32[]{:S(2)}) async-start(bf16[32,8,512]{2,1,0:T(8,128)(2,1)} %output_product.1), calls=%async_computation.5 | async-start | bytes 524288 | tf_op jit(solution)/shard_map/all_to_all | solution.py:443
  219.9 8.2 %all-to-all-done.5.in_ref = bf16[32,8,512]{2,1,0:T(8,128)(2,1)S(1)} async-done(((bf16[32,8,512]{2,1,0:T(8,128)(2,1)}), bf16[32,8,512]{2,1,0:T(8,128)(2,1)S(1)}, u32[]{:S(2)}, u32[]{:S(2)}) %all-to-all-start.5) | async-done | bytes 262176 | tf_op jit(solution)/shard_map/all_to_all | solution.py:443
  228.8 3.1 %panel_order.1 = bf16[32,8,256]{2,1,0:T(8,128)(2,1)} custom-call(s32[128]{0:T(128)} %get-tuple-element.60.from_ref, s32[128]{0:T(128)} %get-tuple-element.61.at_ref, s32[128]{0:T(128)} %get-tuple-element.59.half_ref, bf16[32,8,512]{2,1,0:T(8,128)(2,1)} %copy-done.2), custom_call_target="tpu_custom_call" | custom-call | tf_op jit(solution)/shard_map/panel_order/pallas_call | solution.py:353
  232.0 3.7 %all-to-all-start.6 = ((bf16[32,8,256]{2,1,0:T(8,128)(2,1)}), bf16[32,8,256]{2,1,0:T(8,128)(2,1)S(1)}, u32[]{:S(2)}, u32[]{:S(2)}) async-start(bf16[32,8,256]{2,1,0:T(8,128)(2,1)} %panel_order.1), calls=%async_computation.6 | async-start | bytes 262144 | tf_op jit(solution)/shard_map/all_to_all | solution.py:446
  236.8 6.7 %all-to-all-done.6 = bf16[32,8,256]{2,1,0:T(8,128)(2,1)S(1)} async-done(((bf16[32,8,256]{2,1,0:T(8,128)(2,1)}), bf16[32,8,256]{2,1,0:T(8,128)(2,1)S(1)}, u32[]{:S(2)}, u32[]{:S(2)}) %all-to-all-start.6) | async-done | bytes 131104 | tf_op jit(solution)/shard_map/all_to_all | solution.py:446
  (140 shorter events, 46.9 us)
Async XLA Ops:
  7.2 139.7 %all-gather.3.cloned.1.call-start = ((), (), s32[]{:S(2)}) async-start(), calls=%async_computation.7 | async-start | bytes 10485760 | tf_op jit(solution)/shard_map/all_gather | solution.py:377
  18.0 43.0 %collective-permute-start.11 = (bf16[2,128,1280]{2,1,0:T(8,128)(2,1)}, bf16[2,128,1280]{2,1,0:T(8,128)(2,1)S(1)}, u32[]{:S(2)}, u32[]{:S(2)}) collective-permute-start(bf16[2,128,1280]{2,1,0:T(8,128)(2,1)} %get-tuple-element.36), channel_id=1, source_target_pairs={{0,6},{2,0},{4,2},{6,4},{1,7},{3,1},{5,3},{7,5},{8,14},{10,8},{12,... | collective-permute-start | bytes 1966088 | tf_op jit(solution)/shard_map/ppermute | solution.py:30
  22.6 38.4 %collective-permute-start.12 = (bf16[2,128,1280]{2,1,0:T(8,128)(2,1)}, bf16[2,128,1280]{2,1,0:T(8,128)(2,1)S(1)}, u32[]{:S(2)}, u32[]{:S(2)}) collective-permute-start(bf16[2,128,1280]{2,1,0:T(8,128)(2,1)} %get-tuple-element.37), channel_id=1, source_target_pairs={{0,2},{2,4},{4,6},{6,0},{1,3},{3,5},{5,7},{7,1},{8,10},{10,12},{12... | collective-permute-start | bytes 1966088 | tf_op jit(solution)/shard_map/ppermute | solution.py:30
  23.2 11.6 %all-to-all-start = ((s32[8,1,2]{2,1,0:T(1,128)}), s32[8,1,2]{2,1,0:T(1,128)S(1)}, u32[]{:S(2)}, u32[]{:S(2)}) async-start(s32[8,1,2]{2,1,0:T(1,128)} %broadcast_in_dim.40), calls=%async_computation | async-start | bytes 8192 | tf_op jit(solution)/shard_map/all_to_all | solution.py:384
  28.6 17.8 %collective-permute-start = (bf16[1,128,1280]{2,1,0:T(8,128)(2,1)}, bf16[1,128,1280]{2,1,0:T(8,128)(2,1)}, u32[]{:S(2)}, u32[]{:S(2)}) collective-permute-start(bf16[1,128,1280]{2,1,0:T(8,128)(2,1)} %get-tuple-element.31), channel_id=1, source_target_pairs={{0,2},{2,4},{4,6},{6,0},{1,3},{3,5},{5,7},{7,1},{8,10},{10,12},{12... | collective-permute-start | bytes 983048 | tf_op jit(solution)/shard_map/ppermute | solution.py:30
  28.6 17.8 %collective-permute-start.1 = (bf16[1,128,1280]{2,1,0:T(8,128)(2,1)}, bf16[1,128,1280]{2,1,0:T(8,128)(2,1)}, u32[]{:S(2)}, u32[]{:S(2)}) collective-permute-start(bf16[1,128,1280]{2,1,0:T(8,128)(2,1)} %get-tuple-element.32), channel_id=1, source_target_pairs={{0,6},{2,0},{4,2},{6,4},{1,7},{3,1},{5,3},{7,5},{8,14},{10,8},{12,... | collective-permute-start | bytes 983048 | tf_op jit(solution)/shard_map/ppermute | solution.py:30
  46.5 13.1 %all-to-all-start.1 = ((bf16[4,4,32,256]{3,2,1,0:T(8,128)(2,1)}), bf16[4,4,32,256]{3,2,1,0:T(8,128)(2,1)S(1)}, u32[]{:S(2)}, u32[]{:S(2)}) async-start(bf16[4,4,32,256]{3,2,1,0:T(8,128)(2,1)} %pick_columns.1), calls=%async_computation.1 | async-start | bytes 524288 | tf_op jit(solution)/shard_map/all_to_all | solution.py:397
  50.6 21.5 %collective-permute-start.15 = (bf16[1,128,1280]{2,1,0:T(8,128)(2,1)}, bf16[1,128,1280]{2,1,0:T(8,128)(2,1)S(1)}, u32[]{:S(2)}, u32[]{:S(2)}) collective-permute-start(bf16[1,128,1280]{2,1,0:T(8,128)(2,1)} %collective-permute-done.1), channel_id=1, source_target_pairs={{0,6},{2,0},{4,2},{6,4},{1,7},{3,1},{5,3},{7,5},{8,14},{10,8},{12,... | collective-permute-start | bytes 983048 | tf_op jit(solution)/shard_map/ppermute | solution.py:30
  59.5 12.6 %collective-permute-start.2 = (bf16[16,32,256]{2,1,0:T(8,128)(2,1)S(1)}, bf16[16,32,256]{2,1,0:T(8,128)(2,1)S(1)}, u32[]{:S(2)}, u32[]{:S(2)}) collective-permute-start(bf16[16,32,256]{2,1,0:T(8,128)(2,1)S(1)} %bitcast.70), channel_id=1, source_target_pairs={{0,6},{2,0},{4,2},{6,4},{1,7},{3,1},{5,3},{7,5},{8,14},{10,8},{12,... | collective-permute-start | bytes 786440 | tf_op jit(solution)/shard_map/ppermute | solution.py:30
  60.0 6.8 %collective-permute-start.3 = (bf16[16,32,256]{2,1,0:T(8,128)(2,1)S(1)}, bf16[16,32,256]{2,1,0:T(8,128)(2,1)S(1)}, u32[]{:S(2)}, u32[]{:S(2)}) collective-permute-start(bf16[16,32,256]{2,1,0:T(8,128)(2,1)S(1)} %bitcast.71), channel_id=1, source_target_pairs={{0,2},{2,4},{4,6},{6,0},{1,3},{3,5},{5,7},{7,1},{8,10},{10,12},{12... | collective-permute-start | bytes 786440 | tf_op jit(solution)/shard_map/ppermute | solution.py:30
  61.2 24.4 %collective-permute-start.13 = (bf16[2,128,1280]{2,1,0:T(8,128)(2,1)S(1)}, bf16[2,128,1280]{2,1,0:T(8,128)(2,1)S(1)}, u32[]{:S(2)}, u32[]{:S(2)}) collective-permute-start(bf16[2,128,1280]{2,1,0:T(8,128)(2,1)S(1)} %pad_maximum_fusion), channel_id=1, source_target_pairs={{0,1},{1,0},{2,3},{3,2},{4,5},{5,4},{6,7},{7,6},{8,9},{9,8},{10,11... | collective-permute-start | bytes 1966088 | tf_op jit(solution)/shard_map/ppermute | solution.py:34
  66.8 6.1 %collective-permute-start.4 = (bf16[8,32,256]{2,1,0:T(8,128)(2,1)S(1)}, bf16[8,32,256]{2,1,0:T(8,128)(2,1)S(1)}, u32[]{:S(2)}, u32[]{:S(2)}) collective-permute-start(bf16[8,32,256]{2,1,0:T(8,128)(2,1)S(1)} %slice.56), channel_id=1, source_target_pairs={{0,2},{2,4},{4,6},{6,0},{1,3},{3,5},{5,7},{7,1},{8,10},{10,12},{12... | collective-permute-start | bytes 393224 | tf_op jit(solution)/shard_map/ppermute | solution.py:30
  66.9 15.4 %collective-permute-start.10 = (bf16[1,128,1280]{2,1,0:T(8,128)(2,1)S(1)}, bf16[1,128,1280]{2,1,0:T(8,128)(2,1)S(1)}, u32[]{:S(2)}, u32[]{:S(2)}) collective-permute-start(bf16[1,128,1280]{2,1,0:T(8,128)(2,1)S(1)} %copy-done.16), channel_id=1, source_target_pairs={{0,1},{1,0},{2,3},{3,2},{4,5},{5,4},{6,7},{7,6},{8,9},{9,8},{10,11... | collective-permute-start | bytes 983048 | tf_op jit(solution)/shard_map/ppermute | solution.py:34
  72.1 11.3 %collective-permute-start.14 = (bf16[1,128,1280]{2,1,0:T(8,128)(2,1)}, bf16[1,128,1280]{2,1,0:T(8,128)(2,1)S(1)}, u32[]{:S(2)}, u32[]{:S(2)}) collective-permute-start(bf16[1,128,1280]{2,1,0:T(8,128)(2,1)} %collective-permute-done), channel_id=1, source_target_pairs={{0,2},{2,4},{4,6},{6,0},{1,3},{3,5},{5,7},{7,1},{8,10},{10,12},{12... | collective-permute-start | bytes 983048 | tf_op jit(solution)/shard_map/ppermute | solution.py:30
  72.8 11.2 %collective-permute-start.6 = (bf16[16,32,256]{2,1,0:T(8,128)(2,1)S(1)}, bf16[16,32,256]{2,1,0:T(8,128)(2,1)S(1)}, u32[]{:S(2)}, u32[]{:S(2)}) collective-permute-start(bf16[16,32,256]{2,1,0:T(8,128)(2,1)S(1)} %bitcast.72), channel_id=1, source_target_pairs={{0,1},{1,0},{2,3},{3,2},{4,5},{5,4},{6,7},{7,6},{8,9},{9,8},{10,11... | collective-permute-start | bytes 786440 | tf_op jit(solution)/shard_map/ppermute | solution.py:34
  77.3 6.9 %collective-permute-start.16 = (bf16[1,128,1280]{2,1,0:T(8,128)(2,1)}, bf16[1,128,1280]{2,1,0:T(8,128)(2,1)S(1)}, u32[]{:S(2)}, u32[]{:S(2)}) collective-permute-start(bf16[1,128,1280]{2,1,0:T(8,128)(2,1)} %copy-done.17), channel_id=1, source_target_pairs={{0,1},{1,0},{2,3},{3,2},{4,5},{5,4},{6,7},{7,6},{8,9},{9,8},{10,11... | collective-permute-start | bytes 983048 | tf_op jit(solution)/shard_map/ppermute | solution.py:34
  135.9 10.9 %all-to-all-start.3 = ((bf16[8,8,1280]{2,1,0:T(8,128)(2,1)}), bf16[8,8,1280]{2,1,0:T(8,128)(2,1)S(1)}, u32[]{:S(2)}, u32[]{:S(2)}) async-start(bf16[8,8,1280]{2,1,0:T(8,128)(2,1)} %bitcast.10), calls=%async_computation.3 | async-start | bytes 327680 | tf_op jit(solution)/shard_map/all_to_all | solution.py:419
  141.3 65.5 %all-gather.5.cloned.1.call-start = ((), (), s32[]{:S(2)}) async-start(), calls=%async_computation.8 | async-start | bytes 4325376 | tf_op jit(solution)/shard_map/all_gather | solution.py:436
  163.5 17.4 %all-to-all-start.4 = ((s32[16,1,16]{2,1,0:T(1,128)}), s32[16,1,16]{2,1,0:T(1,128)S(1)}, u32[]{:S(2)}, u32[]{:S(2)}) async-start(s32[16,1,16]{2,1,0:T(1,128)} %broadcast_in_dim.41), calls=%async_computation.4 | async-start | bytes 16384 | tf_op jit(solution)/shard_map/all_to_all | solution.py:439
  175.9 44.0 %collective-permute-start.17 = (bf16[128,2048]{1,0:T(8,128)(2,1)}, bf16[128,2048]{1,0:T(8,128)(2,1)S(1)}, u32[]{:S(2)}, u32[]{:S(2)}) collective-permute-start(bf16[128,2048]{1,0:T(8,128)(2,1)} %get-tuple-element.51), channel_id=1, source_target_pairs={{0,32},{32,64},{64,96},{96,0},{1,33},{33,65},{65,97},{97,1},{2,34}... | collective-permute-start | bytes 1572872 | tf_op jit(solution)/shard_map/ppermute | solution.py:30
  176.1 43.7 %collective-permute-start.18 = (bf16[128,2048]{1,0:T(8,128)(2,1)S(1)}, bf16[128,2048]{1,0:T(8,128)(2,1)S(1)}, u32[]{:S(2)}, u32[]{:S(2)}) collective-permute-start(bf16[128,2048]{1,0:T(8,128)(2,1)S(1)} %get-tuple-element.50), channel_id=1, source_target_pairs={{0,64},{32,96},{64,0},{96,32},{1,65},{33,97},{65,1},{97,33},{2,66}... | collective-permute-start | bytes 1572872 | tf_op jit(solution)/shard_map/ppermute | solution.py:30
  178.8 41.0 %collective-permute-start.19 = (bf16[128,2048]{1,0:T(8,128)(2,1)S(1)}, bf16[128,2048]{1,0:T(8,128)(2,1)S(1)}, u32[]{:S(2)}, u32[]{:S(2)}) collective-permute-start(bf16[128,2048]{1,0:T(8,128)(2,1)S(1)} %get-tuple-element.49), channel_id=1, source_target_pairs={{0,96},{32,0},{64,32},{96,64},{1,97},{33,1},{65,33},{97,65},{2,98}... | collective-permute-start | bytes 1572872 | tf_op jit(solution)/shard_map/ppermute | solution.py:30
  213.8 14.3 %all-to-all-start.5 = ((bf16[32,8,512]{2,1,0:T(8,128)(2,1)}), bf16[32,8,512]{2,1,0:T(8,128)(2,1)S(1)}, u32[]{:S(2)}, u32[]{:S(2)}) async-start(bf16[32,8,512]{2,1,0:T(8,128)(2,1)} %output_product.1), calls=%async_computation.5 | async-start | bytes 524288 | tf_op jit(solution)/shard_map/all_to_all | solution.py:443
  232.0 11.5 %all-to-all-start.6 = ((bf16[32,8,256]{2,1,0:T(8,128)(2,1)}), bf16[32,8,256]{2,1,0:T(8,128)(2,1)S(1)}, u32[]{:S(2)}, u32[]{:S(2)}) async-start(bf16[32,8,256]{2,1,0:T(8,128)(2,1)} %panel_order.1), calls=%async_computation.6 | async-start | bytes 262144 | tf_op jit(solution)/shard_map/all_to_all | solution.py:446
  (29 other events, 230.5 us)
Sparse Core Ops, SparseCore 0:
  18.1 116.3 all-gather.2
  159.8 46.9 all-gather.4
